TPU v7x, 32 devices: a whole 2x2x4 slice. The times are simulated.
32 devices in a mesh: dp: 8 (over z, x), tensor: 4 (over y, core).
Axes of the slice: x: 2, y: 2, z: 4, core: 2. Of those that a mesh axis runs over, the one named last changes fastest.
Arguments:
- tokens: bfloat16 [9216, 2048], P('dp'), may hold values from -6 to 6
- gain_attn: bfloat16 [2048], P('dp'), may hold values from 0.5 to 1.5
- w_query: bfloat16 [2048, 2048], P('dp', 'tensor'), may hold values from -0.125 to 0.125
- w_key: bfloat16 [2048, 256], P('dp', 'tensor'), may hold values from -0.125 to 0.125
- w_value: bfloat16 [2048, 256], P('dp', 'tensor'), may hold values from -0.125 to 0.125
- w_out: bfloat16 [2048, 2048], P('tensor', 'dp'), may hold values from -1 to 1
- gain_mlp: bfloat16 [2048], P('dp'), may hold values from 0.5 to 1.5
- w_gate: bfloat16 [2048, 5632], P('dp', 'tensor'), may hold values from -0.125 to 0.125
- w_up: bfloat16 [2048, 5632], P('dp', 'tensor'), may hold values from -0.125 to 0.125
- w_down: bfloat16 [5632, 2048], P('tensor', 'dp'), may hold values from -0.078125 to 0.078125
- lengths: int32 [8, 4], P('dp'), may hold values from 1 to 1024, 1152 in all within a row
- cotangent: bfloat16 [9216, 2048], P('dp'), may hold values from -6 to 6
Outputs:
- output: bfloat16 [9216, 2048], P('dp')
- grad_tokens: float32 [9216, 2048], P('dp')
- grad_w_query: float32 [2048, 2048], P('dp', 'tensor')
- grad_w_key: float32 [2048, 256], P('dp', 'tensor')
- grad_w_value: float32 [2048, 256], P('dp', 'tensor')
- grad_w_out: float32 [2048, 2048], P('tensor', 'dp')
- grad_w_gate: float32 [2048, 5632], P('dp', 'tensor')
- grad_w_up: float32 [2048, 5632], P('dp', 'tensor')
- grad_w_down: float32 [5632, 2048], P('tensor', 'dp')
- grad_gain_attn: float32 [2048], P('dp')
- grad_gain_mlp: float32 [2048], P('dp')
Inputs may be any that keep to these rules, and one draw needn't show every extreme that they name: Row r lists the lengths of the sequences of data index r, laid one after another in its 1152 tokens; each row sums to 1152 and holds one sequence of 1024.
All inputs are finite; a program needn't handle non-finite values.
Results may differ from a plain program's by a relative error of at most 0.013.
Values may be sent and summed in bfloat16 or wider, within the bound.
A program may use at most 256 MiB of HBM per device.

v0:
```python
import functools

import jax
import jax.numpy as jnp
from jax import lax
from jax.experimental import pallas as pl
from jax.experimental.pallas import tpu as pltpu
from jax.sharding import PartitionSpec as P

HD = 64
QB = 128


def swap_halves(z):
    lane = lax.broadcasted_iota(jnp.int32, z.shape, 1)
    return jnp.where(lane % HD < HD // 2, pltpu.roll(z, 128 - HD // 2, 1), pltpu.roll(z, HD // 2, 1))


def nt(a, b):
    return lax.dot_general(a, b, (((1,), (1,)), ((), ())), preferred_element_type=jnp.float32)


def attn_forward(qkv_ref, cs_ref, sn_ref, start_ref, q_ref, kv_ref, ob_ref, lse_ref, ka, kb, va, vb, between=()):
    tok = qkv_ref.shape[0]
    width = q_ref.shape[1]
    pairs = width // 128
    lane = lax.broadcasted_iota(jnp.int32, (tok, 128), 1)
    cs = cs_ref[...]
    sn = sn_ref[...]
    kv = qkv_ref[:, width:]
    krot = kv * cs + swap_halves(kv) * sn
    kvr = jnp.where(lane < HD, krot, kv).astype(jnp.bfloat16)
    kv_ref[...] = kvr
    kvf = kvr.astype(jnp.float32)
    rolled = pltpu.roll(kvf, HD, 1)
    ka[...] = jnp.where(lane < HD, kvf, 0.0).astype(jnp.bfloat16)
    kb[...] = jnp.where(lane < HD, 0.0, rolled).astype(jnp.bfloat16)
    va[...] = jnp.where(lane < HD, rolled, 0.0).astype(jnp.bfloat16)
    vb[...] = jnp.where(lane < HD, 0.0, kvf).astype(jnp.bfloat16)
    for i in range(tok // QB):
        rows = pl.ds(i * QB, QB)
        kp = (i + 1) * QB
        qs = []
        for p in range(pairs):
            z = qkv_ref[rows, p * 128:(p + 1) * 128]
            r = (z * cs_ref[rows, :] + swap_halves(z) * sn_ref[rows, :]).astype(jnp.bfloat16)
            r = (r.astype(jnp.float32) * 0.125).astype(jnp.bfloat16)
            q_ref[rows, p * 128:(p + 1) * 128] = r
            qs.append(r)
        qe = jnp.concatenate(qs, axis=0)
        col = lax.broadcasted_iota(jnp.int32, (QB, kp), 1)
        row = lax.broadcasted_iota(jnp.int32, (QB, kp), 0) + i * QB
        seen = (col <= row) & (col >= start_ref[rows, :])
        bias = jnp.where(seen, 0.0, -1e30)
        total = 0.0
        lse_tile = jnp.zeros((QB, 128), jnp.float32)
        lane_b = lax.broadcasted_iota(jnp.int32, (QB, 128), 1)
        for odd, (k2, v2) in enumerate(((ka, va), (kb, vb))):
            s = nt(qe, k2[:kp, :]).reshape(pairs, QB, kp) + bias[None]
            m = jnp.max(s, axis=-1, keepdims=True)
            e = jnp.exp(s - m)
            l = jnp.sum(e, axis=-1, keepdims=True)
            o = jnp.dot(e.astype(jnp.bfloat16).reshape(pairs * QB, kp), v2[:kp, :], preferred_element_type=jnp.float32)
            total = total + o.reshape(pairs, QB, 128) / l
            lse = m + jnp.log(l)
            for p in range(pairs):
                lse_tile = jnp.where(lane_b == 2 * p + odd, lse[p], lse_tile)
        for p in range(pairs):
            ob_ref[rows, p * 128:(p + 1) * 128] = total[p].astype(jnp.bfloat16)
        lse_ref[:, i * QB:(i + 1) * QB] = jnp.transpose(lse_tile)[: 2 * pairs]
        if i in between:
            between[i]()


def attn_backward(q_ref, kv_ref, dob_ref, lse_ref, cs_ref, sn_ref, start_ref, out_ref, ka, kb, va, vb, dk, dv, between=()):
    tok, width = q_ref.shape
    pairs = width // 128
    lane = lax.broadcasted_iota(jnp.int32, (tok, 128), 1)
    kvf = kv_ref[...].astype(jnp.float32)
    rolled = pltpu.roll(kvf, HD, 1)
    ka[...] = jnp.where(lane < HD, kvf, 0.0).astype(jnp.bfloat16)
    kb[...] = jnp.where(lane < HD, 0.0, rolled).astype(jnp.bfloat16)
    va[...] = jnp.where(lane < HD, rolled, 0.0).astype(jnp.bfloat16)
    vb[...] = jnp.where(lane < HD, 0.0, kvf).astype(jnp.bfloat16)
    dk[...] = jnp.zeros_like(dk)
    dv[...] = jnp.zeros_like(dv)
    for i in range(tok // QB):
        rows = pl.ds(i * QB, QB)
        kp = (i + 1) * QB
        qe = jnp.concatenate([q_ref[rows, p * 128:(p + 1) * 128] for p in range(pairs)], axis=0)
        de = jnp.concatenate([dob_ref[rows, p * 128:(p + 1) * 128] for p in range(pairs)], axis=0)
        key = lax.broadcasted_iota(jnp.int32, (kp, QB), 0)
        query = lax.broadcasted_iota(jnp.int32, (kp, QB), 1) + i * QB
        seen = (key <= query) & (key >= start_ref[:, i * QB:(i + 1) * QB])
        bias = jnp.where(seen, 0.0, -1e30)
        bias = jnp.concatenate([bias] * pairs, axis=1)
        dq = 0.0
        parts = []
        for odd, (k2, v2) in enumerate(((ka, va), (kb, vb))):
            lse = jnp.concatenate([lse_ref[2 * p + odd:2 * p + odd + 1, i * QB:(i + 1) * QB] for p in range(pairs)], axis=1)
            s = nt(k2[:kp, :], qe)
            pt = jnp.exp(s + bias - lse)
            dp = nt(v2[:kp, :], de)
            delta = jnp.sum(pt * dp, axis=0, keepdims=True)
            ds = (pt * (dp - delta)).astype(jnp.bfloat16)
            dvo = jnp.dot(pt.astype(jnp.bfloat16), de, preferred_element_type=jnp.float32)
            dko = jnp.dot(ds, qe, preferred_element_type=jnp.float32)
            parts.append((dko, dvo))
            dq = dq + lax.dot_general(ds, k2[:kp, :], (((0,), (0,)), ((), ())), preferred_element_type=jnp.float32)
        lk = lane[:kp]
        dk[:kp, :] += jnp.where(lk < HD, parts[0][0], parts[1][0])
        dv[:kp, :] += jnp.where(lk < HD, parts[0][1], parts[1][1])
        cs = cs_ref[rows, :]
        sn = sn_ref[rows, :]
        for p in range(pairs):
            y = dq[p * QB:(p + 1) * QB] * 0.125
            out_ref[rows, p * 128:(p + 1) * 128] = (y * cs - swap_halves(y) * sn).astype(jnp.bfloat16)
        if i in between:
            between[i]()
    dkf = dk[...]
    dkf = dkf + pltpu.roll(dkf, HD, 1)
    dkf = dkf * cs_ref[...] - swap_halves(dkf) * sn_ref[...]
    dvf = dv[...]
    dvf = dvf + pltpu.roll(dvf, HD, 1)
    out_ref[:, width:] = jnp.where(lane < HD, dkf, dvf).astype(jnp.bfloat16)


norm_eps = 1e-05
rope_base = 10000.0
bf16 = jnp.bfloat16
f32 = jnp.float32


def mm(a, b):
    return jnp.dot(a, b, preferred_element_type=f32)


def mm_nt(a, b):
    return lax.dot_general(a, b, (((1,), (1,)), ((), ())), preferred_element_type=f32)


def mm_tn(a, b):
    return lax.dot_general(a, b, (((0,), (0,)), ((), ())), preferred_element_type=f32)


MESH = pl.DeviceIdType.MESH


def ring_place(n, index):
    odd = index % 2
    return (1 - odd) * (index // 2) + odd * (n - 1 - index // 2)


def ring_index(n, place):
    place = (place + 2 * n) % n
    far = place // (n // 2)
    return (1 - far) * 2 * place + far * (2 * (n - 1 - place) + 1)


class Gather:
    def __init__(self, n, chains, send, recv):
        self.n, self.chains, self.send_sem, self.recv_sem = n, chains, send, recv
        self.index = lax.axis_index("dp")
        self.place = ring_place(n, self.index)
        self.up = ring_index(n, self.place + 1)
        self.down = ring_index(n, self.place - 1)
        self.sent, self.events = [], []

    def copy(self, chain, step, way):
        first, whole, *rows = self.chains[chain]
        rows = pl.ds(*rows[way])
        origin = ring_index(self.n, self.place - step if way == 0 else self.place + step)
        place = whole.at[origin, rows]
        return pltpu.make_async_remote_copy(
            src_ref=first.at[rows] if step == 0 else place,
            dst_ref=place,
            send_sem=self.send_sem.at[chain, way, step],
            recv_sem=self.recv_sem.at[chain, way, step],
            device_id={"dp": self.up if way == 0 else self.down},
            device_id_type=MESH,
        )

    def start(self, chain, step):
        for way in (0, 1):
            self.copy(chain, step, way).start()
        self.sent.append((chain, step))

    def order(self, chains):
        self.events += [(chain, step) for step in range(self.n - 1) for chain in chains]

    def pass_on(self, count=1):
        for _ in range(min(count, len(self.events))):
            chain, step = self.events.pop(0)
            for way in (0, 1):
                self.copy(chain, step, way).wait_recv()
            if step + 1 < self.n - 1:
                self.start(chain, step + 1)

    def finish(self):
        for chain, step in self.sent:
            for way in (0, 1):
                self.copy(chain, step, way).wait_send()


def forward_kernel(
    n,
    s_qkv, s_out, s_gate, s_up, s_down, tokens, cotangent, cs_ref, sn_ref, start_ref,
    w_qkv, w_out, w_gate, w_up, w_down, n1_out, q_ref, kv_ref, ob_ref, lse_ref, hid_ref, n2_out, to_gate_out, to_up_out, inner_out, grad_down,
    v_qkv, v_out, n1, n2, qkv, ka, kb, va, vb, part, near, keep, far_part, far, own_n2, weight, stage, inner, grads,
    ring_send, ring_recv, tp_send, tp_recv, local,
):
    tok, width = n1.shape
    block = width // n
    quarter = tok // 4
    sub = quarter // 2
    index = lax.axis_index("dp")
    t = lax.axis_index("tensor")
    c, y = t % 2, t // 2
    mate = y * 2 + (1 - c)
    across = (1 - y) * 2 + c
    h = block // 2
    chains = [
        (s_qkv, v_qkv, (0, h + 16), (h + 16, h)),
        (s_out, v_out, (0, s_out.shape[0] // 2), (s_out.shape[0] // 2, s_out.shape[0] // 2)),
        (s_gate, w_gate, (0, h), (h, h)),
        (s_up, w_up, (0, h), (h, h)),
        (s_down, w_down, (0, h // 2), (h, h // 2)),
        (s_down, w_down, (h // 2, h // 2), (h + h // 2, h // 2)),
    ]
    ring = Gather(n, chains, ring_send, ring_recv)
    barrier = pltpu.get_barrier_semaphore()
    for device in ({"dp": ring.up}, {"dp": ring.down}, {"tensor": mate}, {"tensor": across}):
        pl.semaphore_signal(barrier, inc=1, device_id=device, device_id_type=MESH)

    used = []

    def copy(source, target):
        made = pltpu.make_async_copy(source, target, local.at[len(used)])
        made.start()
        used.append(made)
        return made

    whole = copy(tokens, n2)
    pairs = ((s_qkv, v_qkv), (s_out, v_out), (s_gate, w_gate), (s_up, w_up), (s_down, w_down))
    own = [copy(source, target.at[index]) for source, target in pairs]
    pl.semaphore_wait(barrier, 4)
    ring.start(0, 0)
    ring.start(1, 0)
    ring.order([0, 1])
    whole.wait()
    ring.pass_on(2 * (n - 1) - 2)
    ring.start(2, 0)
    ring.pass_on(1)
    ring.start(3, 0)
    ring.pass_on(1)
    ring.order([2, 3])
    own[0].wait()
    own[1].wait()

    gain_one = v_qkv[:, block : block + 16, :block]
    gain_two = v_qkv[:, block : block + 16, block : 2 * block]
    gains = [[g[i, :1].astype(f32) for i in range(n)] for g in (gain_one, gain_two)]
    gain_one, gain_two = (jnp.concatenate(g, axis=1) for g in gains)
    steps = 4
    rows_each = tok // steps
    for i in range(steps):
        rows = pl.ds(i * rows_each, rows_each)
        z = n2[rows, :].astype(f32)
        inverse = lax.rsqrt(jnp.mean(z * z, axis=-1, keepdims=True) + norm_eps)
        n1[rows, :] = (z * inverse * gain_one).astype(bf16)
        qkv[rows, :] = mm(n1[rows, :], v_qkv[:, :block].reshape(width, qkv.shape[1]))
    saved = [copy(n1, n1_out), copy(v_qkv, w_qkv), copy(v_out, w_out)]
    ring.pass_on()
    attn_forward(qkv, cs_ref, sn_ref, start_ref, q_ref, kv_ref, ob_ref, lse_ref, ka, kb, va, vb, {4: ring.pass_on, 8: ring.pass_on})

    def remote(k, source, target, device):
        made = pltpu.make_async_remote_copy(
            src_ref=source, dst_ref=target, send_sem=tp_send.at[k], recv_sem=tp_recv.at[k],
            device_id={"tensor": device}, device_id_type=MESH,
        )
        made.start()
        return made

    def projected(first):
        rows = pl.ds(pl.multiple_of(first, 16), sub)
        return jnp.concatenate([mm(ob_ref[rows, :], v_out[j]) for j in range(n)], axis=1)

    pieces = [((1 - y) * quarter + i * sub) for i in (0, 1)] + [(y * quarter + i * sub) for i in (0, 1)]
    tp = []
    for i, first in enumerate(pieces):
        part[i * sub : (i + 1) * sub, :] = projected((1 - c) * 2 * quarter + first).astype(bf16)
        tp.append(remote(i, part.at[pl.ds(i * sub, sub)], near.at[pl.ds(i * sub, sub)], mate))
    for i, first in enumerate(pieces):
        mine = projected(c * 2 * quarter + first)
        tp[i].wait_recv()
        total = mine + near[i * sub : (i + 1) * sub, :].astype(f32)
        if i < 2:
            far_part[i * sub : (i + 1) * sub, :] = total.astype(bf16)
            tp.append(remote(4 + i, far_part.at[pl.ds(i * sub, sub)], far.at[pl.ds(i * sub, sub)], across))
        else:
            keep[(i - 2) * sub : (i - 1) * sub, :] = total
    ring.pass_on(2)

    first_row = (2 * c + y) * quarter
    token_rows = copy(tokens.at[pl.ds(pl.multiple_of(first_row, 16), quarter)], own_n2)
    token_rows.wait()
    sent = []
    for i in (0, 1):
        rows = pl.ds(i * sub, sub)
        tp[4 + i].wait_recv()
        hidden = own_n2[rows, :].astype(f32) + keep[rows, :] + far[rows, :].astype(f32)
        hid_ref[rows, :] = hidden
        inverse = lax.rsqrt(jnp.mean(hidden * hidden, axis=-1, keepdims=True) + norm_eps)
        place = pl.ds(pl.multiple_of(first_row + i * sub, 16), sub)
        n2[place, :] = (hidden * inverse * gain_two).astype(bf16)
        sent.append(remote(6 + i, n2.at[place], n2.at[place], across))
        sent.append(remote(8 + i, n2.at[place], n2.at[place], mate))
        ring.pass_on()
    ring.pass_on()
    other_row = (2 * c + 1 - y) * quarter
    for i in (0, 1):
        sent[2 * i].wait_recv()
        place = pl.ds(pl.multiple_of(other_row + i * sub, 16), sub)
        sent.append(remote(10 + i, n2.at[place], n2.at[place], mate))
        ring.pass_on()
    for made in (sent[1], sent[3], sent[4], sent[5]):
        made.wait_recv()
    saved.append(copy(n2, n2_out))
    ring.pass_on(len(ring.events) - 2)
    ring.start(4, 0)
    ring.pass_on(1)
    ring.start(5, 0)
    ring.pass_on(1)
    ring.order([4, 5])
    own[2].wait()
    own[3].wait()

    units = inner.shape[1]
    firsts = list(range(0, units, 256))

    def load(j):
        wide = min(256, units - firsts[j])
        return [
            copy(source.at[:, :, pl.ds(firsts[j], wide)], weight.at[j % 2, k, :, :, pl.ds(0, wide)])
            for k, source in enumerate((w_gate, w_up))
        ]

    loads = {0: load(0)}
    writes = []
    for j, first in enumerate(firsts):
        wide = min(256, units - first)
        if j + 1 < len(firsts):
            loads[j + 1] = load(j + 1)
        for made in loads[j]:
            made.wait()
        gate, up = (mm(n2[...], weight[j % 2, k, :, :, :wide].reshape(width, wide)) for k in (0, 1))
        sig = jax.nn.sigmoid(gate)
        silu = gate * sig
        inner[:, first : first + wide] = (silu * up).astype(bf16)
        if j >= 2:
            for made in writes[j - 2]:
                made.wait()
        stage[j % 2, 0, :, :wide] = (up * (sig * (1.0 + gate * (1.0 - sig)))).astype(bf16)
        stage[j % 2, 1, :, :wide] = silu.astype(bf16)
        writes.append(
            [
                copy(stage.at[j % 2, k, :, pl.ds(0, wide)], target.at[:, pl.ds(first, wide)])
                for k, target in enumerate((to_gate_out, to_up_out))
            ]
        )
        ring.pass_on()
    for made in writes[-2] + writes[-1]:
        made.wait()
    saved.append(copy(inner, inner_out))
    saved[3].wait()
    for made in sent:
        made.wait_send()
    copy(cotangent, n2).wait()
    per = 256 // block
    writes = []
    for j in range(width // 256):
        if j >= 2:
            writes[j - 2].wait()
        grad = mm_tn(n2[:, j * 256 : (j + 1) * 256], inner[...]).astype(bf16)
        grads[j % 2] = grad.reshape(per, block, units)
        writes.append(copy(grads.at[j % 2], grad_down.at[pl.ds(j * per, per)]))
        ring.pass_on()
    writes[-2].wait()
    writes[-1].wait()
    ring.pass_on(len(ring.events))
    for made in tp:
        made.wait_send()
    ring.finish()
    own[4].wait()
    for i, made in enumerate(saved):
        if i != 3:
            made.wait()


def forward(n, s_qkv, s_out, s_gate, s_up, s_down, tokens, cotangent, cs, sn, start):
    tok, width = tokens.shape
    heads = s_qkv.shape[1] - 128
    units = s_gate.shape[1]
    quarter = tok // 4
    vm = pl.BlockSpec(memory_space=pltpu.VMEM)
    anywhere = pl.BlockSpec(memory_space=pl.ANY)
    shards = (s_qkv, s_out, s_gate, s_up, s_down)
    return pl.pallas_call(
        functools.partial(forward_kernel, n),
        out_shape=tuple(jax.ShapeDtypeStruct((n,) + s.shape, bf16) for s in shards)
        + (
            jax.ShapeDtypeStruct((tok, width), bf16),
            jax.ShapeDtypeStruct((tok, heads), bf16),
            jax.ShapeDtypeStruct((tok, 128), bf16),
            jax.ShapeDtypeStruct((tok, heads), bf16),
            jax.ShapeDtypeStruct((heads // HD, tok), f32),
            jax.ShapeDtypeStruct((quarter, width), f32),
            jax.ShapeDtypeStruct((tok, width), bf16),
            jax.ShapeDtypeStruct((tok, units), bf16),
            jax.ShapeDtypeStruct((tok, units), bf16),
            jax.ShapeDtypeStruct((tok, units), bf16),
            jax.ShapeDtypeStruct((n, width // n, units), bf16),
        ),
        in_specs=[anywhere] * 7 + [vm] * 3,
        out_specs=(anywhere,) * 6 + (vm,) * 5 + (anywhere,) * 5,
        scratch_shapes=[
            pltpu.VMEM((n,) + s_qkv.shape, bf16),
            pltpu.VMEM((n,) + s_out.shape, bf16),
            pltpu.VMEM((tok, width), bf16),
            pltpu.VMEM((tok, width), bf16),
            pltpu.VMEM((tok, heads + 128), f32),
            pltpu.VMEM((tok, 128), bf16),
            pltpu.VMEM((tok, 128), bf16),
            pltpu.VMEM((tok, 128), bf16),
            pltpu.VMEM((tok, 128), bf16),
            pltpu.VMEM((2 * quarter, width), bf16),
            pltpu.VMEM((2 * quarter, width), bf16),
            pltpu.VMEM((quarter, width), f32),
            pltpu.VMEM((quarter, width), bf16),
            pltpu.VMEM((quarter, width), bf16),
            pltpu.VMEM((quarter, width), bf16),
            pltpu.VMEM((2, 2, n, width // n, 256), bf16),
            pltpu.VMEM((2, 2, tok, 256), bf16),
            pltpu.VMEM((tok, units), bf16),
            pltpu.VMEM((2, 256 * n // width, width // n, units), bf16),
            pltpu.SemaphoreType.DMA((6, 2, n - 1)),
            pltpu.SemaphoreType.DMA((6, 2, n - 1)),
            pltpu.SemaphoreType.DMA((12,)),
            pltpu.SemaphoreType.DMA((12,)),
            pltpu.SemaphoreType.DMA((64,)),
        ],
        compiler_params=pltpu.CompilerParams(collective_id=1, has_side_effects=True, vmem_limit_bytes=62 * 2**20),
    )(*shards, tokens, cotangent, cs, sn, start)


class Later:
    def __init__(self, make):
        self.make = make

    def start(self):
        self.make().start()

    def wait(self):
        self.make().wait()

    def wait_send(self):
        self.make().wait_send()

    def wait_recv(self):
        self.make().wait_recv()


class Reduce:
    def __init__(self, n, chains, pools, send, recv, slot_sem, term_sem):
        self.n, self.chains, self.pools = n, chains, pools
        self.send_sem, self.recv_sem = send, recv
        self.slot_sem, self.term_sem = slot_sem, term_sem
        self.place = ring_place(n, lax.axis_index("dp"))
        self.up = ring_index(n, self.place + 1)
        self.down = ring_index(n, self.place - 1)
        self.origin = [
            [ring_index(n, self.place - 1 - step), ring_index(n, self.place + 1 + step)] for step in range(n)
        ]
        self.events, self.waiting, self.used = [], [], [0] * len(pools)
        self.busy = [{} for _ in pools]
        self.ready = None

    def send(self, chain, step, way, source):
        return Later(
            lambda: pltpu.make_async_remote_copy(
                src_ref=source(),
                dst_ref=self.landing(chain, step, way),
                send_sem=self.send_sem.at[chain, way, step],
                recv_sem=self.recv_sem.at[chain, way, step],
                device_id={"dp": self.up if way == 0 else self.down},
                device_id_type=MESH,
            )
        )

    def landing(self, chain, step, way):
        slots, rows = self.chains[chain][1], self.chains[chain][2 + way]
        return slots().at[step, way, pl.ds(0, rows[1])]

    def term(self, chain, step, way):
        rows = pl.ds(*self.chains[chain][2 + way])
        return self.chains[chain][0].at[self.origin[step][way], rows]

    def start(self, chain):
        for way in (0, 1):
            made = self.send(chain, 0, way, functools.partial(self.term, chain, 0, way))
            made.start()
            self.waiting.append(made)

    def order(self, chains):
        self.events += [(chain, step) for step in range(self.n - 1) for chain in chains]
        self.fetch()

    def fetch(self):
        if self.ready is not None or not self.events:
            return
        chain, step = self.events[0]
        pool = self.chains[chain][4]
        arrived, terms = self.pools[pool]
        slot = self.used[pool] % arrived.shape[0]
        self.used[pool] += 1
        for made in self.busy[pool].pop(slot, ()):
            made.wait_send()
        copies = []
        for way in (0, 1):
            count = self.chains[chain][2 + way][1]
            copies.append(
                Later(
                    lambda way=way, count=count: pltpu.make_async_copy(
                        self.term(chain, step + 1, way),
                        terms.at[slot, way, pl.ds(0, count)],
                        self.term_sem.at[pool, slot, way],
                    )
                )
            )
            copies[-1].start()
        self.ready = (slot, copies)

    def held(self, pool, slot, way, rows):
        return self.pools[pool][0].at[slot, way, pl.ds(0, rows)]

    def pass_on(self, count=1):
        for _ in range(min(count, len(self.events))):
            chain, step = self.events.pop(0)
            pool, result = self.chains[chain][4:]
            arrived, terms = self.pools[pool]
            slot, copies = self.ready
            self.ready = None
            loads = []
            for way in (0, 1):
                rows = self.chains[chain][2 + way][1]
                self.send(chain, step, way, functools.partial(self.landing, chain, step, way)).wait_recv()
                loads.append(
                    pltpu.make_async_copy(
                        self.landing(chain, step, way),
                        arrived.at[slot, way, pl.ds(0, rows)],
                        self.slot_sem.at[pool, slot, way],
                    )
                )
                loads[-1].start()
            sent = []
            for way in (0, 1):
                rows = self.chains[chain][2 + way][1]
                loads[way].wait()
                copies[way].wait()
                total = arrived[slot, way, :rows].astype(f32) + terms[slot, way, :rows].astype(f32)
                if step + 1 < self.n - 1:
                    arrived[slot, way, :rows] = total.astype(bf16)
                    place = functools.partial(self.held, pool, slot, way, rows)
                    sent.append(self.send(chain, step + 1, way, place))
                    sent[-1].start()
                else:
                    result(way, total)
            self.busy[pool][slot] = sent
            self.fetch()

    def finish(self):
        for busy in self.busy:
            for sent in busy.values():
                for made in sent:
                    made.wait_send()
        for made in self.waiting:
            made.wait_send()


def backward_kernel(
    n,
    g_hbm, n2_hbm, n1_hbm, x_hbm, to_gate, to_up, inner_hbm, grad_down,
    w_qkv, w_out, w_gate, w_up, w_down, q_hbm, kv_hbm, ob_hbm, hid_ref, lse_ref, cs_ref, sn_ref, start_ref,
    output, grad_x, r_down, r_gate, r_up, r_out, r_qkv,
    grad_gate, grad_up, grad_out, grad_qkv, l_down, l_gate, l_up, l_out, l_qkv,
    tile, part, near, far_part, far, keep, dh, gh, rows_in, own_rows, dqkv, stage, stage_o, fin, fin_o, fin_q,
    pool_a, pool_b, pool_c, pool_d, pool_e, pool_f, gain_rows, gain_in, gain_tile,
    ring_send, ring_recv, slot_sem, term_sem, tp_send, tp_recv, credit, local,
):
    tok, width = dh.shape
    block = width // n
    per = 256 // block
    chunks = width // 256
    units = w_gate.shape[2]
    heads = ob_hbm.shape[1]
    quarter = tok // 4
    sub = quarter // 2
    h = block // 2
    ho = heads // 2
    t = lax.axis_index("tensor")
    c, y = t % 2, t // 2
    mate = y * 2 + (1 - c)
    across = (1 - y) * 2 + c
    first_row = (2 * c + y) * quarter
    other_row = (2 * c + 1 - y) * quarter
    count = [0, 0]

    def rows_at(first, rows):
        return pl.ds(pl.multiple_of(first, 16), rows)

    own_rows_at = rows_at(first_row, quarter)
    own_subs = [rows_at(first_row + i * sub, sub) for i in (0, 1)]
    other_subs = [rows_at(other_row + i * sub, sub) for i in (0, 1)]
    sent_half = rows_at((1 - c) * 2 * quarter, 2 * quarter)
    sent_quarter, kept_quarter = rows_at((1 - y) * quarter, quarter), rows_at(y * quarter, quarter)
    sent_tile, kept_tile = (rows_at((2 * c + at) * quarter, quarter) for at in (1 - y, y))

    def now(place):
        return place() if callable(place) else place

    def copy(source, target):
        k = count[0]
        count[0] += 1
        made = Later(lambda: pltpu.make_async_copy(now(source), now(target), local.at[k]))
        made.start()
        return made

    def remote(source, target, device):
        k = count[1]
        count[1] += 1
        return Later(
            lambda: pltpu.make_async_remote_copy(
                src_ref=now(source), dst_ref=now(target), send_sem=tp_send.at[k], recv_sem=tp_recv.at[k],
                device_id={"tensor": device}, device_id_type=MESH,
            )
        )

    def to(result, buffer, writes, firsts):
        def write(way, total):
            if len(writes) >= 2:
                writes[-2].wait()
            rows = total.shape[0]
            slot = len(writes) % 2
            buffer[slot, :rows] = total
            source = lambda: buffer.at[slot, pl.ds(0, rows)]
            writes.append(copy(source, lambda: result.at[pl.ds(firsts[way], rows)]))

        return write

    written = [[], [], []]
    ends = [
        to(r_down, fin, written[0], (0, h)),
        to(r_down, fin, written[0], (h // 2, h + h // 2)),
        to(r_gate, fin, written[0], (0, h)),
        to(r_up, fin, written[0], (0, h)),
        to(r_out, fin_o, written[1], (0, ho)),
        to(r_qkv, fin_q, written[2], (0, h + 16)),
    ]
    chains = [
        (grad_down, lambda: l_down.at[0], (0, h // 2), (h, h // 2), 0, ends[0]),
        (grad_down, lambda: l_down.at[1], (h // 2, h // 2), (h + h // 2, h // 2), 0, ends[1]),
        (grad_gate, lambda: l_gate, (0, h), (h, h), 0, ends[2]),
        (grad_up, lambda: l_up, (0, h), (h, h), 0, ends[3]),
        (grad_out, lambda: l_out, (0, ho), (ho, ho), 1, ends[4]),
        (grad_qkv, lambda: l_qkv, (0, h + 16), (h + 16, h), 2, ends[5]),
    ]
    pools = [(pool_a, pool_b), (pool_c, pool_d), (pool_e, pool_f)]
    ring = Reduce(n, chains, pools, ring_send, ring_recv, slot_sem, term_sem)
    barrier = pltpu.get_barrier_semaphore()
    for device in ({"dp": ring.up}, {"dp": ring.down}, {"tensor": mate}, {"tensor": across}):
        pl.semaphore_signal(barrier, inc=1, device_id=device, device_id_type=MESH)
    gain_load = copy(w_qkv.at[:, pl.ds(block, 16)], gain_tile)
    pl.semaphore_wait(barrier, 4)
    ring.start(0)
    ring.start(1)
    ring.order([0, 1])
    gain_load.wait()
    gains = [
        jnp.concatenate([gain_tile[i, :1, k * block : (k + 1) * block].astype(f32) for i in range(n)], axis=1)
        for k in (0, 1)
    ]

    class Sum:
        def __init__(self, at_once=True):
            self.near, self.far, self.at_once = [], [], at_once

        def put(self, j, value):
            tile[j % 2] = value
            part[j] = tile[j % 2, sent_half, :].astype(bf16)
            self.near.append(remote(lambda: part.at[j], lambda: near.at[j], mate))
            self.near[j].start()
            if j > 0:
                self.absorb(j - 1)
            if j == chunks - 1:
                self.absorb(j)

        def absorb(self, j):
            self.near[j].wait_recv()

            far_part[j] = (tile[j % 2, sent_tile, :] + near[j, sent_quarter, :].astype(f32)).astype(bf16)
            keep[:, j * 256 : (j + 1) * 256] = tile[j % 2, kept_tile, :] + near[j, kept_quarter, :].astype(f32)
            self.far.append(remote(lambda: far_part.at[j], lambda: far.at[j], across))
            if self.at_once:
                self.far[j].start()

        def send_far(self):
            for made in self.far:
                made.start()

        def finish(self):
            for j in range(chunks):
                self.far[j].wait_recv()
                keep[:, j * 256 : (j + 1) * 256] += far[j].astype(f32)
            for made in self.near + self.far:
                made.wait_send()

    class Spread:
        def __init__(self, whole):
            self.whole, self.far, self.near, self.last = whole, [], [], []

        def put(self, i, source):
            place = lambda: self.whole.at[own_subs[i]]
            self.far.append(remote(source, place, across))
            self.far[i].start()
            self.near.append(remote(source, place, mate))
            self.near[i].start()

        def forward(self):
            for i in (0, 1):
                self.far[i].wait_recv()
                place = lambda i=i: self.whole.at[other_subs[i]]
                self.last.append(remote(place, place, mate))
                self.last[i].start()

        def arrive_near(self):
            for made in self.near:
                made.wait_recv()

        def arrive(self):
            for made in self.last:
                made.wait_recv()

        def close(self):
            for made in self.far + self.near + self.last:
                made.wait_send()

    def through_norm(values, gain, base, put):
        gain_grad = 0.0
        for i in (0, 1):
            rows = slice(i * sub, (i + 1) * sub)
            z = values[rows, :].astype(f32)
            inverse = lax.rsqrt(jnp.mean(z * z, axis=-1, keepdims=True) + norm_eps)
            scaled = z * inverse
            grad = keep[rows, :]
            gain_grad = gain_grad + jnp.sum(grad * scaled, axis=0, keepdims=True)
            grad = grad * gain
            grad = inverse * (grad - scaled * jnp.mean(grad * scaled, axis=-1, keepdims=True))
            put(i, rows, base[rows, :].astype(f32) + grad)
        return gain_grad

    def weight_grads(target, left, right):
        writes = []
        cols = right.shape[1]
        for j in range(chunks):
            if j >= 2:
                writes[j - 2].wait()
            grad = mm_tn(left[:, j * 256 : (j + 1) * 256], right[...]).astype(bf16)
            stage[j % 2, :, :, :cols] = grad.reshape(per, block, cols)
            writes.append(copy(stage.at[j % 2, :, :, pl.ds(0, cols)], target.at[pl.ds(j * per, per), pl.ds(0, block)]))
            yield j
        writes[-2].wait()
        writes[-1].wait()

    hid_sum, out_sum, x_sum = Sum(), Sum(False), Sum()
    spread, result, last = Spread(dh), Spread(output), Spread(grad_x)
    gain_rows[...] = jnp.zeros_like(gain_rows)

    def feed_forward(acts, dg, du, weight, wtile):
        loads = [copy(g_hbm, acts), copy(to_gate, dg), copy(to_up, du)]
        firsts = list(range(0, units, 256))

        def tile_load(j):
            wide = min(256, units - firsts[j])
            return copy(w_down.at[:, :, pl.ds(firsts[j], wide)], wtile.at[j % 2, :, :, pl.ds(0, wide)])

        def block_load(j, *sources):
            return [copy(s.at[pl.ds(j * per, per)], weight.at[j % 2, k]) for k, s in enumerate(sources)]

        tiles = [tile_load(0)]
        for made in loads:
            made.wait()
        for j, first in enumerate(firsts):
            wide = min(256, units - first)
            if j + 1 < len(firsts):
                tiles.append(tile_load(j + 1))
            tiles[j].wait()
            grad = mm(acts[...], wtile[j % 2, :, :, :wide].reshape(width, wide))
            cols = slice(first, first + wide)
            dg[:, cols] = (grad * dg[:, cols].astype(f32)).astype(bf16)
            du[:, cols] = (grad * du[:, cols].astype(f32)).astype(bf16)
            if j > 0:
                ring.pass_on()
        acts_load = copy(n2_hbm, acts)
        loads = [block_load(0, w_gate, w_up)]
        for j in range(chunks):
            if j + 1 < chunks:
                loads.append(block_load(j + 1, w_gate, w_up))
            for made in loads[j]:
                made.wait()
            value = mm_nt(dg[...], weight[j % 2, 0].reshape(256, units))
            hid_sum.put(j, value + mm_nt(du[...], weight[j % 2, 1].reshape(256, units)))
            if j % 2 == 1 or j == 4:
                ring.pass_on()
        acts_load.wait()
        for j in weight_grads(grad_gate, acts, dg):
            if j in (2, 5, 7):
                ring.pass_on()
        ring.start(2)
        inner_load = copy(inner_hbm, dg)
        copy(g_hbm.at[own_rows_at], rows_in).wait()
        hid_sum.finish()

        def put(i, rows, grad):
            gh[rows, :] = grad
            place = own_subs[i]
            dh[place, :] = grad.astype(bf16)
            spread.put(i, lambda: dh.at[place])

        gain_rows[1:2, :] = through_norm(hid_ref, gains[1], rows_in, put)
        for j in weight_grads(grad_up, acts, du):
            if j in (2, 5):
                ring.pass_on()
        ring.start(3)
        ring.order([2, 3])
        spread.arrive_near()
        inner_load.wait()
        loads = [block_load(0, w_down)]
        for j in range(chunks):
            if j + 1 < chunks:
                loads.append(block_load(j + 1, w_down))
            loads[j][0].wait()
            out_sum.put(j, mm_nt(dg[...], weight[j % 2, 0].reshape(256, units)))
            if j in (2, 6):
                ring.pass_on()

    pl.run_scoped(
        feed_forward,
        pltpu.VMEM((tok, width), bf16),
        pltpu.VMEM((tok, units), bf16),
        pltpu.VMEM((tok, units), bf16),
        pltpu.VMEM((2, 2, per, block, units), bf16),
        pltpu.VMEM((2, n, block, 256), bf16),
    )
    spread.forward()
    out_sum.send_far()
    ring.pass_on()
    spread.arrive()

    def attention(q, kv, ob, v_out, dob, ka, kb, va, vb, dk, dv):
        loads = [copy(q_hbm, q), copy(kv_hbm, kv), copy(ob_hbm, ob), copy(w_out, v_out)]
        for made in loads:
            made.wait()
        for i in (0, 1):
            rows = slice(2 * i * quarter, 2 * (i + 1) * quarter)
            total = 0.0
            for j in range(n):
                total = total + mm_nt(dh[rows, j * block : (j + 1) * block], v_out[j])
            dob[rows, :] = total.astype(bf16)
        attn_backward(
            q, kv, dob, lse_ref, cs_ref, sn_ref, start_ref, dqkv, ka, kb, va, vb, dk, dv,
            {2: ring.pass_on, 5: ring.pass_on, 8: ring.pass_on},
        )
        writes = []
        for j in range(n):
            if j >= 2:
                writes[j - 2].wait()
            stage_o[j % 2] = mm_tn(ob[...], dh[:, j * block : (j + 1) * block]).astype(bf16)
            writes.append(copy(stage_o.at[j % 2], grad_out.at[j]))
        writes[-2].wait()
        writes[-1].wait()

    pl.run_scoped(
        attention,
        pltpu.VMEM((tok, heads), bf16),
        pltpu.VMEM((tok, 128), bf16),
        pltpu.VMEM((tok, heads), bf16),
        pltpu.VMEM((n, heads, block), bf16),
        pltpu.VMEM((tok, heads), bf16),
        *[pltpu.VMEM((tok, 128), bf16)] * 4,
        *[pltpu.VMEM((tok, 128), f32)] * 2,
    )
    out_sum.finish()
    for i in (0, 1):
        rows = slice(i * sub, (i + 1) * sub)
        own_rows[rows, :] = (hid_ref[rows, :] + keep[rows, :]).astype(bf16)
        result.put(i, lambda i=i: own_rows.at[pl.ds(i * sub, sub)])
    owns = [copy(own_rows, output.at[own_rows_at])]
    for k, device in enumerate((mate, across)):
        pl.semaphore_signal(credit.at[k], inc=1, device_id={"tensor": device}, device_id_type=MESH)
    pl.semaphore_wait(credit.at[0], 1)
    pl.semaphore_wait(credit.at[1], 1)
    ring.pass_on()

    def projections(acts, v_qkv):
        loads = [copy(w_qkv, v_qkv), copy(n1_hbm, acts), copy(x_hbm.at[own_rows_at], rows_in)]
        loads[0].wait()
        for j in range(chunks):
            weight = v_qkv[j * per : (j + 1) * per, :block].reshape(256, heads + 128)
            x_sum.put(j, mm_nt(dqkv[...], weight))
        ring.pass_on()
        loads[1].wait()
        for j in weight_grads(grad_qkv, acts, dqkv):
            if j == 4:
                ring.pass_on()
        loads[2].wait()

    pl.run_scoped(
        projections,
        pltpu.VMEM((tok, width), bf16),
        pltpu.VMEM((n, block + 16, heads + 128), bf16),
    )
    x_sum.finish()

    def put(i, rows, grad):
        rows_in[rows, :] = grad.astype(bf16)
        last.put(i, lambda: rows_in.at[pl.ds(i * sub, sub)])

    gain_rows[0:1, :] = through_norm(rows_in, gains[0], gh, put)
    owns.append(copy(rows_in, grad_x.at[own_rows_at]))
    for k, device in enumerate((mate, across)):
        made = remote(gain_rows, gain_in.at[k], device)
        made.start()
        made.wait()
        gain_rows[...] += gain_in[k]
    for i in range(n):
        both = [gain_rows[k : k + 1, i * block : (i + 1) * block] for k in (0, 1)]
        both = jnp.concatenate(both + [jnp.zeros((1, heads + 128 - 2 * block), f32)], axis=1)
        gain_tile[i] = jnp.broadcast_to(both, (16, heads + 128)).astype(bf16)
    copy(gain_tile, grad_qkv.at[:, pl.ds(block, 16)]).wait()
    result.forward()
    ring.pass_on(len(ring.events) - 2)
    ring.start(4)
    ring.start(5)
    ring.order([4, 5])
    ring.pass_on(2)
    last.forward()
    ring.pass_on(len(ring.events))
    for spreading in (result, last):
        spreading.arrive_near()
        spreading.arrive()
    for spreading in (spread, result, last):
        spreading.close()
    ring.finish()
    for made in owns:
        made.wait()
    for writes in written:
        for made in writes[-2:]:
            made.wait()


def backward(n, g, n2, n1, x, to_gate, to_up, inner, grad_down, w_qkv, w_out, w_gate, w_up, w_down, q, kv, ob, hid, lse, cs, sn, start):
    tok, width = x.shape
    block = width // n
    h = block // 2
    heads, units = ob.shape[1], inner.shape[1]
    quarter = tok // 4
    per, chunks = 256 // block, width // 256
    vm = pl.BlockSpec(memory_space=pltpu.VMEM)
    anywhere = pl.BlockSpec(memory_space=pl.ANY)
    hbm = jax.ShapeDtypeStruct
    qkv = heads + 128
    return pl.pallas_call(
        functools.partial(backward_kernel, n),
        out_shape=(
            hbm((tok, width), bf16),
            hbm((tok, width), bf16),
            hbm((block, units), f32),
            hbm((block, units), f32),
            hbm((block, units), f32),
            hbm((heads, block), f32),
            hbm((block + 16, qkv), f32),
            hbm((n, block, units), bf16),
            hbm((n, block, units), bf16),
            hbm((n, heads, block), bf16),
            hbm((n, block + 16, qkv), bf16),
            hbm((2, n - 1, 2, h // 2, units), bf16),
            hbm((n - 1, 2, h, units), bf16),
            hbm((n - 1, 2, h, units), bf16),
            hbm((n - 1, 2, heads // 2, block), bf16),
            hbm((n - 1, 2, h + 16, qkv), bf16),
        ),
        in_specs=[anywhere] * 16 + [vm] * 5,
        out_specs=(anywhere,) * 16,
        scratch_shapes=[
            pltpu.VMEM((2, tok, 256), f32),
            pltpu.VMEM((chunks, 2 * quarter, 256), bf16),
            pltpu.VMEM((chunks, 2 * quarter, 256), bf16),
            pltpu.VMEM((chunks, quarter, 256), bf16),
            pltpu.VMEM((chunks, quarter, 256), bf16),
            pltpu.VMEM((quarter, width), f32),
            pltpu.VMEM((tok, width), bf16),
            pltpu.VMEM((quarter, width), f32),
            pltpu.VMEM((quarter, width), bf16),
            pltpu.VMEM((quarter, width), bf16),
            pltpu.VMEM((tok, qkv), bf16),
            pltpu.VMEM((2, per, block, units), bf16),
            pltpu.VMEM((2, heads, block), bf16),
            pltpu.VMEM((2, h, units), f32),
            pltpu.VMEM((2, heads // 2, block), f32),
            pltpu.VMEM((2, h + 16, qkv), f32),
            pltpu.VMEM((3, 2, h, units), bf16),
            pltpu.VMEM((3, 2, h, units), bf16),
            pltpu.VMEM((2, 2, heads // 2, block), bf16),
            pltpu.VMEM((2, 2, heads // 2, block), bf16),
            pltpu.VMEM((2, 2, h + 16, qkv), bf16),
            pltpu.VMEM((2, 2, h + 16, qkv), bf16),
            pltpu.VMEM((8, width), f32),
            pltpu.VMEM((2, 8, width), f32),
            pltpu.VMEM((n, 16, qkv), bf16),
            pltpu.SemaphoreType.DMA((6, 2, n - 1)),
            pltpu.SemaphoreType.DMA((6, 2, n - 1)),
            pltpu.SemaphoreType.DMA((3, 3, 2)),
            pltpu.SemaphoreType.DMA((3, 3, 2)),
            pltpu.SemaphoreType.DMA((80,)),
            pltpu.SemaphoreType.DMA((80,)),
            pltpu.SemaphoreType.REGULAR((2,)),
            pltpu.SemaphoreType.DMA((160,)),
        ],
        compiler_params=pltpu.CompilerParams(collective_id=2, has_side_effects=True, vmem_limit_bytes=62 * 2**20),
    )(g, n2, n1, x, to_gate, to_up, inner, grad_down, w_qkv, w_out, w_gate, w_up, w_down, q, kv, ob, hid, lse, cs, sn, start)


def prep_kernel(q_ref, k_ref, v_ref, d_ref, g1_ref, g2_ref, qkv_ref, dt_ref):
    rows, cols = q_ref.shape
    qkv_ref[:rows, :cols] = q_ref[...]
    qkv_ref[:rows, cols:] = jnp.concatenate([k_ref[...], v_ref[...]], axis=1)
    qkv_ref[rows:, :] = jnp.zeros((16, qkv_ref.shape[1]), bf16)
    gains = jnp.concatenate([g1_ref[...], g2_ref[...]], axis=1).astype(f32)
    qkv_ref[rows:, : 2 * rows] = jnp.broadcast_to(gains, (16, 2 * rows)).astype(bf16)
    dt_ref[...] = jnp.transpose(d_ref[...].astype(f32)).astype(bf16)


def prep(w_query, w_key, w_value, w_down, gain_attn, gain_mlp):
    rows, cols = w_query.shape
    vm = pl.BlockSpec(memory_space=pltpu.VMEM)
    return pl.pallas_call(
        prep_kernel,
        out_shape=(
            jax.ShapeDtypeStruct((rows + 16, cols + 128), bf16),
            jax.ShapeDtypeStruct(w_down.shape[::-1], bf16),
        ),
        in_specs=[vm] * 6,
        out_specs=(vm,) * 2,
        compiler_params=pltpu.CompilerParams(vmem_limit_bytes=32 * 2**20),
    )(w_query, w_key, w_value, w_down, gain_attn.reshape(1, -1), gain_mlp.reshape(1, -1))


def per_device(
    n_dp,
    tokens,
    gain_attn,
    w_query,
    w_key,
    w_value,
    w_out,
    gain_mlp,
    w_gate,
    w_up,
    w_down,
    lengths,
    cotangent,
):
    tok, width = tokens.shape
    line = n_dp // 2
    block = width // n_dp
    cols = w_query.shape[1]
    ends = jnp.cumsum(lengths[0], dtype=jnp.int32)
    starts = ends - lengths[0]
    places = jnp.arange(tok, dtype=jnp.int32)
    inside = (places[:, None] >= starts[None, :]) & (places[:, None] < ends[None, :])
    start = jnp.sum(jnp.where(inside, starts[None, :], 0), axis=1, dtype=jnp.int32)
    freqs = rope_base ** (-jnp.arange(HD // 2, dtype=f32) * 2.0 / HD)
    angles = (places - start).astype(f32)[:, None] * freqs[None, :]
    cosine, sine = jnp.cos(angles), jnp.sin(angles)
    cs = jnp.concatenate([cosine] * 4, axis=1)
    sn = jnp.concatenate([-sine, sine, -sine, sine], axis=1)

    p_qkv, p_down = prep(w_query, w_key, w_value, w_down, gain_attn, gain_mlp)
    w_qkv, w_out_all, w_g, w_u, w_d, n1, q, kv, ob, lse, hidden, n2, to_gate, to_up, inner, grad_down = forward(
        n_dp, p_qkv, w_out, w_gate, w_up, p_down, tokens, cotangent, cs, sn, start[:, None]
    )
    output, grad_tokens, s_down, s_gate, s_up, s_out, s_qkv = backward(
        n_dp, cotangent, n2, n1, tokens, to_gate, to_up, inner, grad_down, w_qkv, w_out_all, w_g, w_u, w_d,
        q, kv, ob, hidden, lse, cs, sn, start[None, :]
    )[:7]
    return (
        output,
        grad_tokens.astype(f32),
        s_qkv[:block, :cols],
        s_qkv[:block, cols : cols + HD],
        s_qkv[:block, cols + HD :],
        s_out,
        s_gate,
        s_up,
        s_down.T,
        s_qkv[block, :block],
        s_qkv[block, block : 2 * block],
    )


def solution(mesh):
    placed = (
        P("dp", None),
        P("dp"),
        P("dp", "tensor"),
        P("dp", "tensor"),
        P("dp", "tensor"),
        P("tensor", "dp"),
        P("dp"),
        P("dp", "tensor"),
        P("dp", "tensor"),
        P("tensor", "dp"),
        P("dp", None),
        P("dp", None),
    )
    return jax.shard_map(
        functools.partial(per_device, mesh.shape["dp"]),
        mesh=mesh,
        in_specs=placed,
        out_specs=(
            P("dp", None),
            P("dp", None),
            P("dp", "tensor"),
            P("dp", "tensor"),
            P("dp", "tensor"),
            P("tensor", "dp"),
            P("dp", "tensor"),
            P("dp", "tensor"),
            P("tensor", "dp"),
            P("dp"),
            P("dp"),
        ),
        check_vma=False,
    )
```

profile of v0, /device:TPU:0, one launch (start us, length us, event | category | flops | bytes accessed | tf_op | source)
XLA Modules:
  0.0 584.0 jit_solution(1085451546881940246)
XLA Ops:
  0.6 0.8 reduce-window.4
  1.5 0.7 fusion.2
  2.1 0.7 reshape.51.g1_ref
  2.8 0.7 reshape.52.g2_ref
  3.5 0.1 select_reduce_fusion
  3.6 0.6 broadcast_in_dim.13.start_ref
  4.2 0.9 copy.40.k_ref
  5.0 0.9 copy.41.v_ref
  5.9 1.0 reduce_sum.13.start_ref
  6.9 0.0 copy-start
  6.9 1.1 copy-done
  8.1 0.0 copy-start.3
  8.1 0.9 copy-done.3
  9.0 0.3 shard_map.203
  9.3 0.0 copy-start.1
  9.3 0.8 copy-done.1
  10.2 0.0 copy-start.2
  10.2 0.7 copy-done.2
  10.9 2.1 fusion
  13.0 2.0 pad_maximum_fusion
  15.0 221.0 %shard_map.204 = (bf16[8,272,640]{2,1,0:T(8,128)(2,1)}, bf16[8,512,256]{2,1,0:T(8,128)(2,1)}, bf16[8,256,1408]{2,1,0:T(8,128)(2,1)}, bf16[8,256,1408]{2,1,0:T(8,...) custom-call(bf16[272,640]{1,0:T(8,128)(2,1)} %copy-done.2, ...), custom_call_target="tpu_custom_call" | custom-call | tf_op jit(solution)/shard_map/pallas_call | solution.py:408
  236.1 326.4 %shard_map.205 = (bf16[1152,2048]{1,0:T(8,128)(2,1)}, bf16[1152,2048]{1,0:T(8,128)(2,1)}, f32[256,1408]{1,0:T(8,128)}, f32[256,1408]{1,0:T(8,128)}, f32[256,1408...) custom-call(bf16[1152,2048]{1,0:T(8,128)(2,1)} %g_hbm.1, ...), custom_call_target="tpu_custom_call" | custom-call | tf_op jit(solution)/shard_map/pallas_call | solution.py:982
  562.5 1.3 fusion.3
  563.8 1.1 fusion.4
  564.8 1.9 slice.15
  566.7 0.7 copy.45
  567.4 0.7 copy.44
  568.1 0.0 slice-start
  568.1 3.0 copy.46
  571.1 0.0 slice-start.1
  571.1 7.5 %convert_element_type.11 = f32[1152,2048]{1,0:T(8,128)} convert(bf16[1152,2048]{1,0:T(8,128)(2,1)} %get-tuple-element.55) | non-fusion elementwise | flops 2359296 | bytes 14155776 | tf_op jit(solution)/shard_map/convert_element_type | solution.py:1108
  578.5 0.0 slice-done
  578.5 0.0 slice-done.1
  578.5 0.0 copy-start.6
  578.6 0.0 copy-start.5
  578.6 2.3 copy.51
  580.8 0.0 copy-done.6
  580.8 0.0 copy-start.4
  580.8 0.8 copy.52
  581.6 0.0 copy-done.5
  581.6 1.1 copy.53
  582.7 0.0 copy-done.4
  582.7 1.1 copy.54
  (3 shorter events, 0.0 us)
Async XLA Ops:
  6.9 1.1 copy-start
  8.1 0.9 copy-start.3
  9.3 0.9 copy-start.1
  10.2 0.7 copy-start.2
  568.1 10.4 %slice-start = ((s8[4718592]{0:T(1024)(128)(4,1)}), s8[524288]{0:T(1024)(128)(4,1)S(1)}, s32[]{:S(2)}) async-start(s8[4718592]{0:T(1024)(128)(4,1)} %bitcast.11), calls=%async_computation | async-start | bytes 1048576
  571.1 7.5 %slice-start.1 = ((s8[4718592]{0:T(1024)(128)(4,1)}), s8[4194304]{0:T(1024)(128)(4,1)S(1)}, s32[]{:S(2)}) async-start(s8[4718592]{0:T(1024)(128)(4,1)} %bitcast.11), calls=%async_computation.1 | async-start | bytes 8388608
  578.5 2.3 copy-start.6
  578.6 3.1 copy-start.5
  580.8 1.9 copy-start.4
where the time goes:
time: 594 us; the launch traced here: 584 us
  Pallas kernels  548 us (92%)
  local copies, waits for them, and re-layouts  22.2 us (4%)
  other arithmetic  13.2 us (2%)
    pallas_call x1, Pallas kernels, backward(): pl.pallas_call(functools.partial(backward_kernel, n), out_shape=(hbm((tok...  326 us
    pallas_call x1, Pallas kernels, forward(): pl.pallas_call(functools.partial(forward_kernel, n), out_shape=tuple((jax...  221 us
    unnamed x27, local copies, waits for them, and re-layouts  15 us

commit v1 on v0

--- a/solution.py
+++ b/solution.py
@@ -160,19 +160,19 @@
 class Gather:
     def __init__(self, n, chains, send, recv):
         self.n, self.chains, self.send_sem, self.recv_sem = n, chains, send, recv
-        self.index = lax.axis_index("dp")
-        self.place = ring_place(n, self.index)
+        self.place = ring_place(n, lax.axis_index("dp"))
         self.up = ring_index(n, self.place + 1)
         self.down = ring_index(n, self.place - 1)
-        self.sent, self.events = [], []
+        self.sent, self.events, self.groups = [], [], []
 
     def copy(self, chain, step, way):
-        first, whole, *rows = self.chains[chain]
+        first, whole, cols, *rows = self.chains[chain]
         rows = pl.ds(*rows[way])
+        cols = () if cols is None else (pl.ds(*cols),)
         origin = ring_index(self.n, self.place - step if way == 0 else self.place + step)
-        place = whole.at[origin, rows]
+        place = whole.at[(origin, rows) + cols]
         return pltpu.make_async_remote_copy(
-            src_ref=first.at[rows] if step == 0 else place,
+            src_ref=first.at[(rows,) + cols] if step == 0 else place,
             dst_ref=place,
             send_sem=self.send_sem.at[chain, way, step],
             recv_sem=self.recv_sem.at[chain, way, step],
@@ -185,16 +185,31 @@
             self.copy(chain, step, way).start()
         self.sent.append((chain, step))
 
-    def order(self, chains):
-        self.events += [(chain, step) for step in range(self.n - 1) for chain in chains]
+    def queue(self, chains):
+        self.groups.append(chains)
+        self.begin()
+
+    def begin(self):
+        if self.groups and len(self.events) <= 1:
+            chains = self.groups.pop(0)
+            for chain in chains:
+                self.start(chain, 0)
+            self.events += [(chain, step) for step in range(self.n - 1) for chain in chains]
 
     def pass_on(self, count=1):
-        for _ in range(min(count, len(self.events))):
+        for _ in range(count):
+            if not self.events:
+                return
             chain, step = self.events.pop(0)
             for way in (0, 1):
                 self.copy(chain, step, way).wait_recv()
             if step + 1 < self.n - 1:
                 self.start(chain, step + 1)
+            self.begin()
+
+    def through(self, chains):
+        while any(chain in chains for chain, _ in self.events) or any(set(g) & set(chains) for g in self.groups):
+            self.pass_on()
 
     def finish(self):
         for chain, step in self.sent:
@@ -205,27 +220,30 @@
 def forward_kernel(
     n,
     s_qkv, s_out, s_gate, s_up, s_down, tokens, cotangent, cs_ref, sn_ref, start_ref,
-    w_qkv, w_out, w_gate, w_up, w_down, n1_out, q_ref, kv_ref, ob_ref, lse_ref, hid_ref, n2_out, to_gate_out, to_up_out, inner_out, grad_down,
-    v_qkv, v_out, n1, n2, qkv, ka, kb, va, vb, part, near, keep, far_part, far, own_n2, weight, stage, inner, grads,
-    ring_send, ring_recv, tp_send, tp_recv, local,
+    w_qkv, w_out, w_gate, w_up, w_down, n1_out, q_ref, kv_ref, ob_ref, lse_ref, hid_ref,
+    n2_out, to_gate_out, to_up_out, inner_out, grad_down, dg_out, du_out, dn2_out,
+    v_qkv, v_out, n1, n2, part, near, keep, far_part, far, own_n2, ring_send, ring_recv, tp_send, tp_recv, local,
 ):
     tok, width = n1.shape
     block = width // n
     quarter = tok // 4
     sub = quarter // 2
+    units = s_gate.shape[1]
+    early = to_early(units)
     index = lax.axis_index("dp")
     t = lax.axis_index("tensor")
     c, y = t % 2, t // 2
     mate = y * 2 + (1 - c)
     across = (1 - y) * 2 + c
     h = block // 2
-    chains = [
-        (s_qkv, v_qkv, (0, h + 16), (h + 16, h)),
-        (s_out, v_out, (0, s_out.shape[0] // 2), (s_out.shape[0] // 2, s_out.shape[0] // 2)),
-        (s_gate, w_gate, (0, h), (h, h)),
-        (s_up, w_up, (0, h), (h, h)),
-        (s_down, w_down, (0, h // 2), (h, h // 2)),
-        (s_down, w_down, (h // 2, h // 2), (h + h // 2, h // 2)),
+    ho = s_out.shape[0] // 2
+    chains = [(s_qkv, v_qkv, None, (0, h + 16), (h + 16, h)), (s_out, v_out, None, (0, ho), (ho, ho))]
+    for cols in ((0, early), (early, units - early)):
+        for shard, whole in ((s_gate, w_gate), (s_up, w_up), (s_down, w_down)):
+            chains.append((shard, whole, cols, (0, h), (h, h)))
+    chains[-1:] = [
+        (s_down, w_down, (early, units - early), (0, h // 2), (h, h // 2)),
+        (s_down, w_down, (early, units - early), (h // 2, h // 2), (h + h // 2, h // 2)),
     ]
     ring = Gather(n, chains, ring_send, ring_recv)
     barrier = pltpu.get_barrier_semaphore()
@@ -244,16 +262,12 @@
     pairs = ((s_qkv, v_qkv), (s_out, v_out), (s_gate, w_gate), (s_up, w_up), (s_down, w_down))
     own = [copy(source, target.at[index]) for source, target in pairs]
     pl.semaphore_wait(barrier, 4)
-    ring.start(0, 0)
-    ring.start(1, 0)
-    ring.order([0, 1])
+    ring.queue([0, 1])
+    ring.queue([2, 3, 4])
+    ring.queue([5, 6])
+    ring.queue([7, 8])
     whole.wait()
-    ring.pass_on(2 * (n - 1) - 2)
-    ring.start(2, 0)
-    ring.pass_on(1)
-    ring.start(3, 0)
-    ring.pass_on(1)
-    ring.order([2, 3])
+    ring.through([0, 1])
     own[0].wait()
     own[1].wait()
 
@@ -261,17 +275,27 @@
     gain_two = v_qkv[:, block : block + 16, block : 2 * block]
     gains = [[g[i, :1].astype(f32) for i in range(n)] for g in (gain_one, gain_two)]
     gain_one, gain_two = (jnp.concatenate(g, axis=1) for g in gains)
-    steps = 4
-    rows_each = tok // steps
-    for i in range(steps):
-        rows = pl.ds(i * rows_each, rows_each)
-        z = n2[rows, :].astype(f32)
-        inverse = lax.rsqrt(jnp.mean(z * z, axis=-1, keepdims=True) + norm_eps)
-        n1[rows, :] = (z * inverse * gain_one).astype(bf16)
-        qkv[rows, :] = mm(n1[rows, :], v_qkv[:, :block].reshape(width, qkv.shape[1]))
+
+    def attention(qkv, ka, kb, va, vb):
+        steps = 4
+        rows_each = tok // steps
+        for i in range(steps):
+            rows = pl.ds(i * rows_each, rows_each)
+            z = n2[rows, :].astype(f32)
+            inverse = lax.rsqrt(jnp.mean(z * z, axis=-1, keepdims=True) + norm_eps)
+            n1[rows, :] = (z * inverse * gain_one).astype(bf16)
+            qkv[rows, :] = mm(n1[rows, :], v_qkv[:, :block].reshape(width, qkv.shape[1]))
+            if i in (1, 3):
+                ring.pass_on()
+        attn_forward(
+            qkv, cs_ref, sn_ref, start_ref, q_ref, kv_ref, ob_ref, lse_ref, ka, kb, va, vb,
+            {i: ring.pass_on for i in (2, 4, 6, 8)},
+        )
+
+    pl.run_scoped(
+        attention, pltpu.VMEM((tok, v_qkv.shape[2]), f32), *[pltpu.VMEM((tok, 128), bf16)] * 4
+    )
     saved = [copy(n1, n1_out), copy(v_qkv, w_qkv), copy(v_out, w_out)]
-    ring.pass_on()
-    attn_forward(qkv, cs_ref, sn_ref, start_ref, q_ref, kv_ref, ob_ref, lse_ref, ka, kb, va, vb, {4: ring.pass_on, 8: ring.pass_on})
 
     def remote(k, source, target, device):
         made = pltpu.make_async_remote_copy(
@@ -299,7 +323,8 @@
             tp.append(remote(4 + i, far_part.at[pl.ds(i * sub, sub)], far.at[pl.ds(i * sub, sub)], across))
         else:
             keep[(i - 2) * sub : (i - 1) * sub, :] = total
-    ring.pass_on(2)
+        if i == 1:
+            ring.pass_on()
 
     first_row = (2 * c + y) * quarter
     token_rows = copy(tokens.at[pl.ds(pl.multiple_of(first_row, 16), quarter)], own_n2)
@@ -307,6 +332,7 @@
     sent = []
     for i in (0, 1):
         rows = pl.ds(i * sub, sub)
+        ring.pass_on(3)
         tp[4 + i].wait_recv()
         hidden = own_n2[rows, :].astype(f32) + keep[rows, :] + far[rows, :].astype(f32)
         hid_ref[rows, :] = hidden
@@ -315,92 +341,153 @@
         n2[place, :] = (hidden * inverse * gain_two).astype(bf16)
         sent.append(remote(6 + i, n2.at[place], n2.at[place], across))
         sent.append(remote(8 + i, n2.at[place], n2.at[place], mate))
-        ring.pass_on()
-    ring.pass_on()
+    saved[0].wait()
+    cot_load = copy(cotangent, n1)
     other_row = (2 * c + 1 - y) * quarter
     for i in (0, 1):
+        ring.pass_on(3)
         sent[2 * i].wait_recv()
         place = pl.ds(pl.multiple_of(other_row + i * sub, 16), sub)
         sent.append(remote(10 + i, n2.at[place], n2.at[place], mate))
-        ring.pass_on()
     for made in (sent[1], sent[3], sent[4], sent[5]):
         made.wait_recv()
     saved.append(copy(n2, n2_out))
-    ring.pass_on(len(ring.events) - 2)
-    ring.start(4, 0)
-    ring.pass_on(1)
-    ring.start(5, 0)
-    ring.pass_on(1)
-    ring.order([4, 5])
-    own[2].wait()
-    own[3].wait()
-
-    units = inner.shape[1]
-    firsts = list(range(0, units, 256))
-
-    def load(j):
-        wide = min(256, units - firsts[j])
-        return [
-            copy(source.at[:, :, pl.ds(firsts[j], wide)], weight.at[j % 2, k, :, :, pl.ds(0, wide)])
-            for k, source in enumerate((w_gate, w_up))
-        ]
-
-    loads = {0: load(0)}
-    writes = []
-    for j, first in enumerate(firsts):
-        wide = min(256, units - first)
-        if j + 1 < len(firsts):
-            loads[j + 1] = load(j + 1)
-        for made in loads[j]:
+    ring.through([2, 3, 4])
+    cot_load.wait()
+    for made in own[2:]:
+        made.wait()
+    per = 256 // block
+    chunks = width // 256
+
+    def feed_forward(weight, stage, inner, dg, du, blocks, sums, grads):
+        tiles = [(first, min(256, units - first)) for first in range(0, units, 256)]
+        before = early // 256
+
+        def load(j):
+            first, wide = tiles[j]
+            sources = (w_gate, w_up, w_down) if j < before else (w_gate, w_up)
+            return [
+                copy(source.at[:, :, pl.ds(first, wide)], weight.at[j % 2, k, :, :, pl.ds(0, wide)])
+                for k, source in enumerate(sources)
+            ]
+
+        def tile(j, k, rows):
+            wide = tiles[j][1]
+            return mm(rows[...], weight[j % 2, k, :, :, :wide].reshape(width, wide))
+
+        def gated(j):
+            first, wide = tiles[j]
+            gate, up = tile(j, 0, n2), tile(j, 1, n2)
+            sig = jax.nn.sigmoid(gate)
+            silu = gate * sig
+            inner[:, first : first + wide] = (silu * up).astype(bf16)
+            return up * (sig * (1.0 + gate * (1.0 - sig))), silu
+
+        def weight_grads(target, rows, right, calls):
+            cols = right.shape[1]
+            writes = []
+            for j in range(chunks):
+                if j >= 2:
+                    writes[j - 2].wait()
+                grad = mm_tn(rows[:, j * 256 : (j + 1) * 256], right[...]).astype(bf16)
+                grads[j % 2, :, :, :cols] = grad.reshape(per, block, cols)
+                writes.append(copy(grads.at[j % 2, :, :, pl.ds(0, cols)], target.at[pl.ds(j * per, per)]))
+                if j in calls:
+                    ring.pass_on()
+            writes[-2].wait()
+            writes[-1].wait()
+
+        loads = [load(0)]
+        for j in range(before):
+            if j + 1 < before:
+                loads.append(load(j + 1))
+            for made in loads[j]:
+                made.wait()
+            to_gate, to_up = gated(j)
+            ring.pass_on()
+            first, wide = tiles[j]
+            grad = tile(j, 2, n1)
+            dg[:, first : first + wide] = (grad * to_gate).astype(bf16)
+            du[:, first : first + wide] = (grad * to_up).astype(bf16)
+            ring.pass_on()
+
+        def block_load(j):
+            return [
+                copy(s.at[pl.ds(j * per, per), :, pl.ds(0, early)], blocks.at[j % 2, k])
+                for k, s in enumerate((w_gate, w_up))
+            ]
+
+        loads = [block_load(0)]
+        writes = []
+        for j in range(chunks):
+            if j + 1 < chunks:
+                loads.append(block_load(j + 1))
+            for made in loads[j]:
+                made.wait()
+            if j >= 2:
+                writes[j - 2].wait()
+            value = mm_nt(dg[...], blocks[j % 2, 0].reshape(256, early))
+            sums[j % 2] = value + mm_nt(du[...], blocks[j % 2, 1].reshape(256, early))
+            writes.append(copy(sums.at[j % 2], dn2_out.at[j]))
+            if j % 2 == 1:
+                ring.pass_on()
+        for made in writes[-2:]:
             made.wait()
-        gate, up = (mm(n2[...], weight[j % 2, k, :, :, :wide].reshape(width, wide)) for k in (0, 1))
-        sig = jax.nn.sigmoid(gate)
-        silu = gate * sig
-        inner[:, first : first + wide] = (silu * up).astype(bf16)
-        if j >= 2:
-            for made in writes[j - 2]:
+        early_writes = [copy(dg, dg_out), copy(du, du_out)]
+        ring.through([5, 6])
+        loads = {before: load(before)}
+        writes = []
+        for j in range(before, len(tiles)):
+            if j + 1 < len(tiles):
+                loads[j + 1] = load(j + 1)
+            for made in loads[j]:
                 made.wait()
-        stage[j % 2, 0, :, :wide] = (up * (sig * (1.0 + gate * (1.0 - sig)))).astype(bf16)
-        stage[j % 2, 1, :, :wide] = silu.astype(bf16)
-        writes.append(
-            [
-                copy(stage.at[j % 2, k, :, pl.ds(0, wide)], target.at[:, pl.ds(first, wide)])
-                for k, target in enumerate((to_gate_out, to_up_out))
-            ]
-        )
-        ring.pass_on()
-    for made in writes[-2] + writes[-1]:
-        made.wait()
-    saved.append(copy(inner, inner_out))
-    saved[3].wait()
+            first, wide = tiles[j]
+            for k, value in enumerate(gated(j)):
+                if len(writes) >= 4:
+                    writes[-4].wait()
+                stage[j % 2, k, :, :wide] = value.astype(bf16)
+                target = (to_gate_out, to_up_out)[k]
+                writes.append(copy(stage.at[j % 2, k, :, pl.ds(0, wide)], target.at[:, pl.ds(first - early, wide)]))
+            ring.pass_on(2)
+        for made in writes[-4:]:
+            made.wait()
+        inner_write = copy(inner, inner_out)
+        weight_grads(grad_down, n1, inner, range(chunks))
+        inner_write.wait()
+        for made in early_writes:
+            made.wait()
+
+    pl.run_scoped(
+        feed_forward,
+        pltpu.VMEM((2, 3, n, block, 256), bf16),
+        pltpu.VMEM((2, 2, tok, 256), bf16),
+        pltpu.VMEM((tok, units), bf16),
+        pltpu.VMEM((tok, early), bf16),
+        pltpu.VMEM((tok, early), bf16),
+        pltpu.VMEM((2, 2, per, block, early), bf16),
+        pltpu.VMEM((2, tok, 256), f32),
+        pltpu.VMEM((2, per, block, units), bf16),
+    )
+    ring.pass_on(len(ring.events))
     for made in sent:
         made.wait_send()
-    copy(cotangent, n2).wait()
-    per = 256 // block
-    writes = []
-    for j in range(width // 256):
-        if j >= 2:
-            writes[j - 2].wait()
-        grad = mm_tn(n2[:, j * 256 : (j + 1) * 256], inner[...]).astype(bf16)
-        grads[j % 2] = grad.reshape(per, block, units)
-        writes.append(copy(grads.at[j % 2], grad_down.at[pl.ds(j * per, per)]))
-        ring.pass_on()
-    writes[-2].wait()
-    writes[-1].wait()
-    ring.pass_on(len(ring.events))
     for made in tp:
         made.wait_send()
     ring.finish()
-    own[4].wait()
-    for i, made in enumerate(saved):
-        if i != 3:
-            made.wait()
+    for made in saved[1:]:
+        made.wait()
+
+
+def to_early(units):
+    return (units // 256 + 1) // 2 * 256
 
 
 def forward(n, s_qkv, s_out, s_gate, s_up, s_down, tokens, cotangent, cs, sn, start):
     tok, width = tokens.shape
     heads = s_qkv.shape[1] - 128
     units = s_gate.shape[1]
+    early = to_early(units)
     quarter = tok // 4
     vm = pl.BlockSpec(memory_space=pltpu.VMEM)
     anywhere = pl.BlockSpec(memory_space=pl.ANY)
@@ -416,38 +503,32 @@
             jax.ShapeDtypeStruct((heads // HD, tok), f32),
             jax.ShapeDtypeStruct((quarter, width), f32),
             jax.ShapeDtypeStruct((tok, width), bf16),
-            jax.ShapeDtypeStruct((tok, units), bf16),
-            jax.ShapeDtypeStruct((tok, units), bf16),
+            jax.ShapeDtypeStruct((tok, units - early), bf16),
+            jax.ShapeDtypeStruct((tok, units - early), bf16),
             jax.ShapeDtypeStruct((tok, units), bf16),
             jax.ShapeDtypeStruct((n, width // n, units), bf16),
+            jax.ShapeDtypeStruct((tok, early), bf16),
+            jax.ShapeDtypeStruct((tok, early), bf16),
+            jax.ShapeDtypeStruct((width // 256, tok, 256), f32),
         ),
         in_specs=[anywhere] * 7 + [vm] * 3,
-        out_specs=(anywhere,) * 6 + (vm,) * 5 + (anywhere,) * 5,
+        out_specs=(anywhere,) * 6 + (vm,) * 5 + (anywhere,) * 8,
         scratch_shapes=[
             pltpu.VMEM((n,) + s_qkv.shape, bf16),
             pltpu.VMEM((n,) + s_out.shape, bf16),
             pltpu.VMEM((tok, width), bf16),
             pltpu.VMEM((tok, width), bf16),
-            pltpu.VMEM((tok, heads + 128), f32),
-            pltpu.VMEM((tok, 128), bf16),
-            pltpu.VMEM((tok, 128), bf16),
-            pltpu.VMEM((tok, 128), bf16),
-            pltpu.VMEM((tok, 128), bf16),
             pltpu.VMEM((2 * quarter, width), bf16),
             pltpu.VMEM((2 * quarter, width), bf16),
             pltpu.VMEM((quarter, width), f32),
             pltpu.VMEM((quarter, width), bf16),
             pltpu.VMEM((quarter, width), bf16),
             pltpu.VMEM((quarter, width), bf16),
-            pltpu.VMEM((2, 2, n, width // n, 256), bf16),
-            pltpu.VMEM((2, 2, tok, 256), bf16),
-            pltpu.VMEM((tok, units), bf16),
-            pltpu.VMEM((2, 256 * n // width, width // n, units), bf16),
-            pltpu.SemaphoreType.DMA((6, 2, n - 1)),
-            pltpu.SemaphoreType.DMA((6, 2, n - 1)),
+            pltpu.SemaphoreType.DMA((9, 2, n - 1)),
+            pltpu.SemaphoreType.DMA((9, 2, n - 1)),
             pltpu.SemaphoreType.DMA((12,)),
             pltpu.SemaphoreType.DMA((12,)),
-            pltpu.SemaphoreType.DMA((64,)),
+            pltpu.SemaphoreType.DMA((128,)),
         ],
         compiler_params=pltpu.CompilerParams(collective_id=1, has_side_effects=True, vmem_limit_bytes=62 * 2**20),
     )(*shards, tokens, cotangent, cs, sn, start)
@@ -481,9 +562,9 @@
         self.origin = [
             [ring_index(n, self.place - 1 - step), ring_index(n, self.place + 1 + step)] for step in range(n)
         ]
-        self.events, self.waiting, self.used = [], [], [0] * len(pools)
+        self.events, self.groups, self.waiting, self.used = [], [], [], [0] * len(pools)
         self.busy = [{} for _ in pools]
-        self.ready = None
+        self.ready = self.pending = None
 
     def send(self, chain, step, way, source):
         return Later(
@@ -498,12 +579,18 @@
         )
 
     def landing(self, chain, step, way):
-        slots, rows = self.chains[chain][1], self.chains[chain][2 + way]
-        return slots().at[step, way, pl.ds(0, rows[1])]
+        (slots, first), rows = self.chains[chain][2], self.chains[chain][3 + way]
+        return slots.at[first + (step, way, pl.ds(0, rows[1]))]
 
     def term(self, chain, step, way):
-        rows = pl.ds(*self.chains[chain][2 + way])
-        return self.chains[chain][0].at[self.origin[step][way], rows]
+        terms, cols = self.chains[chain][:2]
+        rows = pl.ds(*self.chains[chain][3 + way])
+        cols = () if cols is None else (pl.ds(*cols),)
+        return terms.at[(self.origin[step][way], rows) + cols]
+
+    def part(self, chain, way):
+        cols = self.chains[chain][1]
+        return (pl.ds(0, self.chains[chain][3 + way][1]),) + (() if cols is None else (pl.ds(0, cols[1]),))
 
     def start(self, chain):
         for way in (0, 1):
@@ -511,15 +598,34 @@
             made.start()
             self.waiting.append(made)
 
-    def order(self, chains):
-        self.events += [(chain, step) for step in range(self.n - 1) for chain in chains]
+    def queue(self, chains):
+        self.groups.append(chains)
+        self.begin()
+
+    def add(self, chain, events=None):
+        self.start(chain)
+        if events is None:
+            before, after, self.events = self.events, [(chain, step) for step in range(self.n - 1)], []
+            while before:
+                self.events += before[:1] + after[:1]
+                before, after = before[1:], after[1:]
+            events = after
+        self.events += events
         self.fetch()
+
+    def begin(self):
+        if self.groups and len(self.events) <= 4:
+            chains = self.groups.pop(0)
+            for chain in chains:
+                self.start(chain)
+            self.events += [(chain, step) for step in range(self.n - 1) for chain in chains]
+            self.fetch()
 
     def fetch(self):
         if self.ready is not None or not self.events:
             return
         chain, step = self.events[0]
-        pool = self.chains[chain][4]
+        pool = self.chains[chain][5]
         arrived, terms = self.pools[pool]
         slot = self.used[pool] % arrived.shape[0]
         self.used[pool] += 1
@@ -527,12 +633,11 @@
             made.wait_send()
         copies = []
         for way in (0, 1):
-            count = self.chains[chain][2 + way][1]
             copies.append(
                 Later(
-                    lambda way=way, count=count: pltpu.make_async_copy(
+                    lambda way=way: pltpu.make_async_copy(
                         self.term(chain, step + 1, way),
-                        terms.at[slot, way, pl.ds(0, count)],
+                        terms.at[(slot, way) + self.part(chain, way)],
                         self.term_sem.at[pool, slot, way],
                     )
                 )
@@ -540,43 +645,70 @@
             copies[-1].start()
         self.ready = (slot, copies)
 
-    def held(self, pool, slot, way, rows):
-        return self.pools[pool][0].at[slot, way, pl.ds(0, rows)]
+    def held(self, chain, way, slot):
+        return self.pools[self.chains[chain][5]][0].at[(slot, way) + self.part(chain, way)]
 
     def pass_on(self, count=1):
-        for _ in range(min(count, len(self.events))):
+        for _ in range(count):
+            if not self.events:
+                return
+            self.flush()
             chain, step = self.events.pop(0)
-            pool, result = self.chains[chain][4:]
-            arrived, terms = self.pools[pool]
+            pool = self.chains[chain][5]
             slot, copies = self.ready
             self.ready = None
             loads = []
             for way in (0, 1):
-                rows = self.chains[chain][2 + way][1]
                 self.send(chain, step, way, functools.partial(self.landing, chain, step, way)).wait_recv()
-                loads.append(
-                    pltpu.make_async_copy(
-                        self.landing(chain, step, way),
-                        arrived.at[slot, way, pl.ds(0, rows)],
-                        self.slot_sem.at[pool, slot, way],
-                    )
-                )
+                loads.append(self.load(chain, step, way, pool, slot))
                 loads[-1].start()
-            sent = []
-            for way in (0, 1):
-                rows = self.chains[chain][2 + way][1]
-                loads[way].wait()
-                copies[way].wait()
-                total = arrived[slot, way, :rows].astype(f32) + terms[slot, way, :rows].astype(f32)
-                if step + 1 < self.n - 1:
-                    arrived[slot, way, :rows] = total.astype(bf16)
-                    place = functools.partial(self.held, pool, slot, way, rows)
-                    sent.append(self.send(chain, step + 1, way, place))
-                    sent[-1].start()
-                else:
-                    result(way, total)
-            self.busy[pool][slot] = sent
+            self.pending = (chain, step, slot, copies, loads)
             self.fetch()
+            self.begin()
+
+    def load(self, chain, step, way, pool, slot):
+        return Later(
+            lambda: pltpu.make_async_copy(
+                self.landing(chain, step, way), self.held(chain, way, slot), self.slot_sem.at[pool, slot, way]
+            )
+        )
+
+    def flush(self):
+        if self.pending is None:
+            return
+        chain, step, slot, copies, loads = self.pending
+        self.pending = None
+        pool, result = self.chains[chain][5:]
+        arrived, terms = self.pools[pool]
+        sent = []
+        for way in (0, 1):
+            loads[way].wait()
+            copies[way].wait()
+            place = (slot, way) + self.part(chain, way)
+            total = arrived[place].astype(f32) + terms[place].astype(f32)
+            if step + 1 < self.n - 1:
+                arrived[place] = total.astype(arrived.dtype)
+                sent.append(self.send(chain, step + 1, way, functools.partial(self.held, chain, way, slot)))
+                sent[-1].start()
+            else:
+                result(way, total)
+        self.busy[pool][slot] = sent
+
+    def turn(self, due):
+        if due:
+            self.pass_on()
+        else:
+            self.flush()
+
+    def hop(self, due=True):
+        if due:
+            self.pass_on()
+            self.flush()
+
+    def drain(self):
+        while self.events or self.groups:
+            self.pass_on()
+        self.flush()
 
     def finish(self):
         for busy in self.busy:
@@ -589,12 +721,12 @@
 
 def backward_kernel(
     n,
-    g_hbm, n2_hbm, n1_hbm, x_hbm, to_gate, to_up, inner_hbm, grad_down,
+    g_hbm, n2_hbm, n1_hbm, x_hbm, to_gate, to_up, inner_hbm, grad_down, early_dg, early_du, early_dn2,
     w_qkv, w_out, w_gate, w_up, w_down, q_hbm, kv_hbm, ob_hbm, hid_ref, lse_ref, cs_ref, sn_ref, start_ref,
-    output, grad_x, r_down, r_gate, r_up, r_out, r_qkv,
-    grad_gate, grad_up, grad_out, grad_qkv, l_down, l_gate, l_up, l_out, l_qkv,
-    tile, part, near, far_part, far, keep, dh, gh, rows_in, own_rows, dqkv, stage, stage_o, fin, fin_o, fin_q,
-    pool_a, pool_b, pool_c, pool_d, pool_e, pool_f, gain_rows, gain_in, gain_tile,
+    output, grad_x, r_down, r_gate, r_up, r_out, r_qkv, r_gain,
+    grad_gate, grad_up, grad_out, grad_qkv, grad_gain, l_down, l_gate, l_up, l_out, l_qkv, l_gain,
+    tile, part, near, far_part, far, keep, dh, gh, rows_in, own_rows, dqkv, stage, stage_o, fin, fin_o, fin_q, gain_sum,
+    pool_a, pool_b, pool_c, pool_d, pool_e, pool_f, pool_g, pool_h, gain_rows, gain_in, gain_tile, gain_out,
     ring_send, ring_recv, slot_sem, term_sem, tp_send, tp_recv, credit, local,
 ):
     tok, width = dh.shape
@@ -611,6 +743,7 @@
     c, y = t % 2, t // 2
     mate = y * 2 + (1 - c)
     across = (1 - y) * 2 + c
+    diagonal = (1 - y) * 2 + (1 - c)
     first_row = (2 * c + y) * quarter
     other_row = (2 * c + 1 - y) * quarter
     count = [0, 0]
@@ -622,8 +755,8 @@
     own_subs = [rows_at(first_row + i * sub, sub) for i in (0, 1)]
     other_subs = [rows_at(other_row + i * sub, sub) for i in (0, 1)]
     sent_half = rows_at((1 - c) * 2 * quarter, 2 * quarter)
+    sent_tile, kept_tile = (rows_at((2 * c + at) * quarter, quarter) for at in (1 - y, y))
     sent_quarter, kept_quarter = rows_at((1 - y) * quarter, quarter), rows_at(y * quarter, quarter)
-    sent_tile, kept_tile = (rows_at((2 * c + at) * quarter, quarter) for at in (1 - y, y))
 
     def now(place):
         return place() if callable(place) else place
@@ -645,50 +778,47 @@
             )
         )
 
-    def to(result, buffer, writes, firsts):
+    def to(result, buffer, writes, firsts, cols=None):
         def write(way, total):
             if len(writes) >= 2:
                 writes[-2].wait()
-            rows = total.shape[0]
+            rows = pl.ds(0, total.shape[0])
             slot = len(writes) % 2
-            buffer[slot, :rows] = total
-            source = lambda: buffer.at[slot, pl.ds(0, rows)]
-            writes.append(copy(source, lambda: result.at[pl.ds(firsts[way], rows)]))
+            lanes = () if cols is None else (pl.ds(0, cols[1]),)
+            buffer[(slot, rows) + lanes] = total
+            target = (pl.ds(firsts[way], total.shape[0]),) + (() if cols is None else (pl.ds(*cols),))
+            writes.append(copy(lambda: buffer.at[(slot, rows) + lanes], lambda: result.at[target]))
 
         return write
 
+    early = to_early(units)
+    def gain_done(way, total):
+        if way == 0:
+            gain_sum[...] = total
+
     written = [[], [], []]
-    ends = [
-        to(r_down, fin, written[0], (0, h)),
-        to(r_down, fin, written[0], (h // 2, h + h // 2)),
-        to(r_gate, fin, written[0], (0, h)),
-        to(r_up, fin, written[0], (0, h)),
-        to(r_out, fin_o, written[1], (0, ho)),
-        to(r_qkv, fin_q, written[2], (0, h + 16)),
+    chains = [
+        (grad_down, None, (l_down, (0,)), (0, h // 2), (h, h // 2), 0, to(r_down, fin, written[0], (0, h))),
+        (
+            grad_down, None, (l_down, (1,)), (h // 2, h // 2), (h + h // 2, h // 2), 0,
+            to(r_down, fin, written[0], (h // 2, h + h // 2)),
+        ),
+        (grad_gate, None, (l_gate, ()), (0, h), (h, h), 0, to(r_gate, fin, written[0], (0, h))),
+        (grad_up, None, (l_up, ()), (0, h), (h, h), 0, to(r_up, fin, written[0], (0, h))),
+        (grad_out, None, (l_out, ()), (0, ho), (ho, ho), 1, to(r_out, fin_o, written[1], (0, ho))),
+        (grad_qkv, None, (l_qkv, ()), (0, h), (h, h), 2, to(r_qkv, fin_q, written[2], (0, h))),
+        (grad_gain, None, (l_gain, ()), (0, 8), (8, 8), 3, gain_done),
     ]
-    chains = [
-        (grad_down, lambda: l_down.at[0], (0, h // 2), (h, h // 2), 0, ends[0]),
-        (grad_down, lambda: l_down.at[1], (h // 2, h // 2), (h + h // 2, h // 2), 0, ends[1]),
-        (grad_gate, lambda: l_gate, (0, h), (h, h), 0, ends[2]),
-        (grad_up, lambda: l_up, (0, h), (h, h), 0, ends[3]),
-        (grad_out, lambda: l_out, (0, ho), (ho, ho), 1, ends[4]),
-        (grad_qkv, lambda: l_qkv, (0, h + 16), (h + 16, h), 2, ends[5]),
-    ]
-    pools = [(pool_a, pool_b), (pool_c, pool_d), (pool_e, pool_f)]
+    pools = [(pool_a, pool_b), (pool_c, pool_d), (pool_e, pool_f), (pool_g, pool_h)]
     ring = Reduce(n, chains, pools, ring_send, ring_recv, slot_sem, term_sem)
     barrier = pltpu.get_barrier_semaphore()
-    for device in ({"dp": ring.up}, {"dp": ring.down}, {"tensor": mate}, {"tensor": across}):
+    for device in ({"dp": ring.up}, {"dp": ring.down}, {"tensor": mate}, {"tensor": across}, {"tensor": diagonal}):
         pl.semaphore_signal(barrier, inc=1, device_id=device, device_id_type=MESH)
     gain_load = copy(w_qkv.at[:, pl.ds(block, 16)], gain_tile)
-    pl.semaphore_wait(barrier, 4)
-    ring.start(0)
-    ring.start(1)
-    ring.order([0, 1])
-    gain_load.wait()
-    gains = [
-        jnp.concatenate([gain_tile[i, :1, k * block : (k + 1) * block].astype(f32) for i in range(n)], axis=1)
-        for k in (0, 1)
-    ]
+
+    def gain(k):
+        parts = [gain_tile[i, :1, k * block : (k + 1) * block].astype(f32) for i in range(n)]
+        return jnp.concatenate(parts, axis=1)
 
     class Sum:
         def __init__(self, at_once=True):
@@ -706,7 +836,6 @@
 
         def absorb(self, j):
             self.near[j].wait_recv()
-
             far_part[j] = (tile[j % 2, sent_tile, :] + near[j, sent_quarter, :].astype(f32)).astype(bf16)
             keep[:, j * 256 : (j + 1) * 256] = tile[j % 2, kept_tile, :] + near[j, kept_quarter, :].astype(f32)
             self.far.append(remote(lambda: far_part.at[j], lambda: far.at[j], across))
@@ -716,9 +845,11 @@
         def send_far(self):
             for made in self.far:
                 made.start()
-
-        def finish(self):
+            self.at_once = True
+
+        def finish(self, due=()):
             for j in range(chunks):
+                ring.turn(j in due)
                 self.far[j].wait_recv()
                 keep[:, j * 256 : (j + 1) * 256] += far[j].astype(f32)
             for made in self.near + self.far:
@@ -735,8 +866,10 @@
             self.near.append(remote(source, place, mate))
             self.near[i].start()
 
-        def forward(self):
+        def forward(self, calls):
             for i in (0, 1):
+                ring.pass_on(calls[i])
+                ring.flush()
                 self.far[i].wait_recv()
                 place = lambda i=i: self.whole.at[other_subs[i]]
                 self.last.append(remote(place, place, mate))
@@ -776,7 +909,7 @@
                 writes[j - 2].wait()
             grad = mm_tn(left[:, j * 256 : (j + 1) * 256], right[...]).astype(bf16)
             stage[j % 2, :, :, :cols] = grad.reshape(per, block, cols)
-            writes.append(copy(stage.at[j % 2, :, :, pl.ds(0, cols)], target.at[pl.ds(j * per, per), pl.ds(0, block)]))
+            writes.append(copy(stage.at[j % 2, :, :, pl.ds(0, cols)], target.at[pl.ds(j * per, per)]))
             yield j
         writes[-2].wait()
         writes[-1].wait()
@@ -785,73 +918,92 @@
     spread, result, last = Spread(dh), Spread(output), Spread(grad_x)
     gain_rows[...] = jnp.zeros_like(gain_rows)
 
-    def feed_forward(acts, dg, du, weight, wtile):
-        loads = [copy(g_hbm, acts), copy(to_gate, dg), copy(to_up, du)]
-        firsts = list(range(0, units, 256))
+    def feed_forward(acts, dg, du, weight, sums, wtile):
+        late = units - early
+        tiles = [(first, min(256, units - first)) for first in range(early, units, 256)]
 
         def tile_load(j):
-            wide = min(256, units - firsts[j])
-            return copy(w_down.at[:, :, pl.ds(firsts[j], wide)], wtile.at[j % 2, :, :, pl.ds(0, wide)])
-
-        def block_load(j, *sources):
-            return [copy(s.at[pl.ds(j * per, per)], weight.at[j % 2, k]) for k, s in enumerate(sources)]
-
-        tiles = [tile_load(0)]
-        for made in loads:
-            made.wait()
-        for j, first in enumerate(firsts):
-            wide = min(256, units - first)
-            if j + 1 < len(firsts):
-                tiles.append(tile_load(j + 1))
-            tiles[j].wait()
+            first, wide = tiles[j]
+            return copy(w_down.at[:, :, pl.ds(first, wide)], wtile.at[j % 2, :, :, pl.ds(0, wide)])
+
+        def late_load(j):
+            made = [
+                copy(s.at[pl.ds(j * per, per), :, pl.ds(early, late)], weight.at[j % 2, k, :, :, pl.ds(0, late)])
+                for k, s in enumerate((w_gate, w_up))
+            ]
+            return made + [copy(early_dn2.at[j], sums.at[j % 2])]
+
+        def block_load(j):
+            return copy(w_down.at[pl.ds(j * per, per)], weight.at[j % 2, 0])
+
+        acts_load = copy(g_hbm, acts)
+        tile_loads = [tile_load(0)]
+        factors = [copy(to_gate, dg.at[:, pl.ds(early, late)]), copy(to_up, du.at[:, pl.ds(early, late)])]
+        loads = [late_load(0)]
+        row_load = copy(g_hbm.at[own_rows_at], rows_in)
+        firsts = [copy(early_dg, dg.at[:, pl.ds(0, early)]), copy(early_du, du.at[:, pl.ds(0, early)])]
+        pl.semaphore_wait(barrier, 5)
+        ring.queue([0, 1])
+        acts_load.wait()
+        for j, (first, wide) in enumerate(tiles):
+            if j + 1 < len(tiles):
+                tile_loads.append(tile_load(j + 1))
+            tile_loads[j].wait()
             grad = mm(acts[...], wtile[j % 2, :, :, :wide].reshape(width, wide))
+            if j == 0:
+                for made in factors:
+                    made.wait()
             cols = slice(first, first + wide)
             dg[:, cols] = (grad * dg[:, cols].astype(f32)).astype(bf16)
             du[:, cols] = (grad * du[:, cols].astype(f32)).astype(bf16)
-            if j > 0:
-                ring.pass_on()
-        acts_load = copy(n2_hbm, acts)
-        loads = [block_load(0, w_gate, w_up)]
+            ring.hop(j > 0)
         for j in range(chunks):
             if j + 1 < chunks:
-                loads.append(block_load(j + 1, w_gate, w_up))
+                loads.append(late_load(j + 1))
+            if j == 0:
+                acts_load = copy(n2_hbm, acts)
             for made in loads[j]:
                 made.wait()
-            value = mm_nt(dg[...], weight[j % 2, 0].reshape(256, units))
-            hid_sum.put(j, value + mm_nt(du[...], weight[j % 2, 1].reshape(256, units)))
-            if j % 2 == 1 or j == 4:
-                ring.pass_on()
+
+            value = mm_nt(dg[:, early:], weight[j % 2, 0, :, :, :late].reshape(256, late))
+            value = value + mm_nt(du[:, early:], weight[j % 2, 1, :, :, :late].reshape(256, late))
+            hid_sum.put(j, value + sums[j % 2])
+            ring.hop(j % 3 != 2)
+        loads = [block_load(0)]
         acts_load.wait()
-        for j in weight_grads(grad_gate, acts, dg):
-            if j in (2, 5, 7):
-                ring.pass_on()
-        ring.start(2)
-        inner_load = copy(inner_hbm, dg)
-        copy(g_hbm.at[own_rows_at], rows_in).wait()
-        hid_sum.finish()
-
+        for made in firsts:
+            made.wait()
         def put(i, rows, grad):
             gh[rows, :] = grad
             place = own_subs[i]
             dh[place, :] = grad.astype(bf16)
             spread.put(i, lambda: dh.at[place])
 
-        gain_rows[1:2, :] = through_norm(hid_ref, gains[1], rows_in, put)
+        for j in weight_grads(grad_gate, acts, dg):
+            ring.hop(j in (1, 4, 6))
+            if j == 3:
+                gain_load.wait()
+                row_load.wait()
+                hid_sum.finish()
+                gain_rows[1:2, :] = through_norm(hid_ref, gain(1), rows_in, put)
+                ring.hop()
+        inner_load = copy(inner_hbm, dg)
+        ring.add(2, [(2, 0), (2, 1)])
         for j in weight_grads(grad_up, acts, du):
-            if j in (2, 5):
-                ring.pass_on()
-        ring.start(3)
-        ring.order([2, 3])
+            ring.turn(j in (1, 3, 6))
+        steps = n - 1
+        ring.add(3, [pair for s in range(steps) for pair in ((3, s), (2, s + 2)) if pair[1] < steps])
         spread.arrive_near()
         inner_load.wait()
-        loads = [block_load(0, w_down)]
         for j in range(chunks):
             if j + 1 < chunks:
-                loads.append(block_load(j + 1, w_down))
-            loads[j][0].wait()
+                loads.append(block_load(j + 1))
+            loads[j].wait()
             out_sum.put(j, mm_nt(dg[...], weight[j % 2, 0].reshape(256, units)))
-            if j in (2, 6):
-                ring.pass_on()
+            ring.turn(j in (1, 3, 5))
+            if j == 6:
+                spread.forward((1, 0))
+                out_sum.send_far()
 
     pl.run_scoped(
         feed_forward,
@@ -859,102 +1011,101 @@
         pltpu.VMEM((tok, units), bf16),
         pltpu.VMEM((tok, units), bf16),
         pltpu.VMEM((2, 2, per, block, units), bf16),
+        pltpu.VMEM((2, tok, 256), f32),
         pltpu.VMEM((2, n, block, 256), bf16),
     )
-    spread.forward()
-    out_sum.send_far()
-    ring.pass_on()
+    ring.turn(True)
     spread.arrive()
-
-    def attention(q, kv, ob, v_out, dob, ka, kb, va, vb, dk, dv):
-        loads = [copy(q_hbm, q), copy(kv_hbm, kv), copy(ob_hbm, ob), copy(w_out, v_out)]
-        for made in loads:
-            made.wait()
+    ring.turn(False)
+
+    def attention(q, kv, ob, v_out, v_qkv, dob, ka, kb, va, vb, dk, dv):
+        pairs = ((w_out, v_out), (q_hbm, q), (kv_hbm, kv), (w_qkv, v_qkv), (ob_hbm, ob))
+        loads = [copy(source, target) for source, target in pairs]
+        loads[0].wait()
         for i in (0, 1):
             rows = slice(2 * i * quarter, 2 * (i + 1) * quarter)
             total = 0.0
             for j in range(n):
                 total = total + mm_nt(dh[rows, j * block : (j + 1) * block], v_out[j])
             dob[rows, :] = total.astype(bf16)
+        loads[1].wait()
+        loads[2].wait()
         attn_backward(
             q, kv, dob, lse_ref, cs_ref, sn_ref, start_ref, dqkv, ka, kb, va, vb, dk, dv,
-            {2: ring.pass_on, 5: ring.pass_on, 8: ring.pass_on},
+            {i: functools.partial(ring.turn, i in (1, 3, 6, 8)) for i in range(tok // QB)},
         )
+        out_sum.finish()
+        own_rows[...] = (hid_ref[...] + keep[...]).astype(bf16)
+        for k, device in enumerate((mate, across)):
+            pl.semaphore_signal(credit.at[k], inc=1, device_id={"tensor": device}, device_id_type=MESH)
+        loads[3].wait()
+        loads[4].wait()
+        pl.semaphore_wait(credit.at[0], 1)
+        pl.semaphore_wait(credit.at[1], 1)
+        for j in range(chunks):
+            weight = v_qkv[j * per : (j + 1) * per, :block].reshape(256, heads + 128)
+            x_sum.put(j, mm_nt(dqkv[...], weight))
+            ring.turn(j in (2, 6))
         writes = []
         for j in range(n):
             if j >= 2:
                 writes[j - 2].wait()
             stage_o[j % 2] = mm_tn(ob[...], dh[:, j * block : (j + 1) * block]).astype(bf16)
             writes.append(copy(stage_o.at[j % 2], grad_out.at[j]))
+            ring.turn(j in (2, n - 2))
         writes[-2].wait()
         writes[-1].wait()
 
+    row_load = copy(x_hbm.at[own_rows_at], rows_in)
     pl.run_scoped(
         attention,
         pltpu.VMEM((tok, heads), bf16),
         pltpu.VMEM((tok, 128), bf16),
         pltpu.VMEM((tok, heads), bf16),
         pltpu.VMEM((n, heads, block), bf16),
+        pltpu.VMEM((n, block + 16, heads + 128), bf16),
         pltpu.VMEM((tok, heads), bf16),
         *[pltpu.VMEM((tok, 128), bf16)] * 4,
         *[pltpu.VMEM((tok, 128), f32)] * 2,
     )
-    out_sum.finish()
-    for i in (0, 1):
-        rows = slice(i * sub, (i + 1) * sub)
-        own_rows[rows, :] = (hid_ref[rows, :] + keep[rows, :]).astype(bf16)
-        result.put(i, lambda i=i: own_rows.at[pl.ds(i * sub, sub)])
     owns = [copy(own_rows, output.at[own_rows_at])]
-    for k, device in enumerate((mate, across)):
-        pl.semaphore_signal(credit.at[k], inc=1, device_id={"tensor": device}, device_id_type=MESH)
-    pl.semaphore_wait(credit.at[0], 1)
-    pl.semaphore_wait(credit.at[1], 1)
-    ring.pass_on()
-
-    def projections(acts, v_qkv):
-        loads = [copy(w_qkv, v_qkv), copy(n1_hbm, acts), copy(x_hbm.at[own_rows_at], rows_in)]
-        loads[0].wait()
-        for j in range(chunks):
-            weight = v_qkv[j * per : (j + 1) * per, :block].reshape(256, heads + 128)
-            x_sum.put(j, mm_nt(dqkv[...], weight))
-        ring.pass_on()
-        loads[1].wait()
+
+    def projections(acts):
+        copy(n1_hbm, acts).wait()
         for j in weight_grads(grad_qkv, acts, dqkv):
-            if j == 4:
-                ring.pass_on()
-        loads[2].wait()
-
-    pl.run_scoped(
-        projections,
-        pltpu.VMEM((tok, width), bf16),
-        pltpu.VMEM((n, block + 16, heads + 128), bf16),
-    )
-    x_sum.finish()
+            ring.turn(j in (2, 6))
+            if j == 2:
+                for i in (0, 1):
+                    result.put(i, lambda i=i: own_rows.at[pl.ds(i * sub, sub)])
+
+    pl.run_scoped(projections, pltpu.VMEM((tok, width), bf16))
+    ring.queue([4, 5])
+    row_load.wait()
+    x_sum.finish((1, 4, 7))
 
     def put(i, rows, grad):
         rows_in[rows, :] = grad.astype(bf16)
         last.put(i, lambda: rows_in.at[pl.ds(i * sub, sub)])
 
-    gain_rows[0:1, :] = through_norm(rows_in, gains[0], gh, put)
+    gain_rows[0:1, :] = through_norm(rows_in, gain(0), gh, put)
     owns.append(copy(rows_in, grad_x.at[own_rows_at]))
-    for k, device in enumerate((mate, across)):
-        made = remote(gain_rows, gain_in.at[k], device)
-        made.start()
-        made.wait()
-        gain_rows[...] += gain_in[k]
     for i in range(n):
         both = [gain_rows[k : k + 1, i * block : (i + 1) * block] for k in (0, 1)]
-        both = jnp.concatenate(both + [jnp.zeros((1, heads + 128 - 2 * block), f32)], axis=1)
-        gain_tile[i] = jnp.broadcast_to(both, (16, heads + 128)).astype(bf16)
-    copy(gain_tile, grad_qkv.at[:, pl.ds(block, 16)]).wait()
-    result.forward()
-    ring.pass_on(len(ring.events) - 2)
-    ring.start(4)
-    ring.start(5)
-    ring.order([4, 5])
-    ring.pass_on(2)
-    last.forward()
-    ring.pass_on(len(ring.events))
+        gain_out[i] = jnp.broadcast_to(jnp.concatenate(both, axis=1), (16, 2 * block))
+    copy(gain_out, grad_gain).wait()
+    ring.turn(True)
+    ring.add(6)
+    result.forward((1, 3))
+    last.forward((4, 4))
+    ring.drain()
+    gain_in[t] = gain_sum[...]
+    shares = [remote(gain_sum, gain_in.at[t], device) for device in (mate, across, diagonal)]
+    for made in shares:
+        made.start()
+    for made in shares:
+        made.wait()
+    gain_sum[...] = (gain_in[0] + gain_in[1]) + (gain_in[2] + gain_in[3])
+    owns.append(copy(gain_sum, r_gain))
     for spreading in (result, last):
         spreading.arrive_near()
         spreading.arrive()
@@ -968,7 +1119,7 @@
             made.wait()
 
 
-def backward(n, g, n2, n1, x, to_gate, to_up, inner, grad_down, w_qkv, w_out, w_gate, w_up, w_down, q, kv, ob, hid, lse, cs, sn, start):
+def backward(n, g, n2, n1, x, to_gate, to_up, inner, grads, w_qkv, w_out, w_gate, w_up, w_down, q, kv, ob, hid, lse, cs, sn, start):
     tok, width = x.shape
     block = width // n
     h = block // 2
@@ -988,19 +1139,22 @@
             hbm((block, units), f32),
             hbm((block, units), f32),
             hbm((heads, block), f32),
-            hbm((block + 16, qkv), f32),
+            hbm((block, qkv), f32),
+            hbm((8, 2 * block), f32),
             hbm((n, block, units), bf16),
             hbm((n, block, units), bf16),
             hbm((n, heads, block), bf16),
-            hbm((n, block + 16, qkv), bf16),
+            hbm((n, block, qkv), bf16),
+            hbm((n, 16, 2 * block), f32),
             hbm((2, n - 1, 2, h // 2, units), bf16),
             hbm((n - 1, 2, h, units), bf16),
             hbm((n - 1, 2, h, units), bf16),
             hbm((n - 1, 2, heads // 2, block), bf16),
-            hbm((n - 1, 2, h + 16, qkv), bf16),
+            hbm((n - 1, 2, h, qkv), bf16),
+            hbm((n - 1, 2, 8, 2 * block), f32),
         ),
-        in_specs=[anywhere] * 16 + [vm] * 5,
-        out_specs=(anywhere,) * 16,
+        in_specs=[anywhere] * 19 + [vm] * 5,
+        out_specs=(anywhere,) * 19,
         scratch_shapes=[
             pltpu.VMEM((2, tok, 256), f32),
             pltpu.VMEM((chunks, 2 * quarter, 256), bf16),
@@ -1017,27 +1171,31 @@
             pltpu.VMEM((2, heads, block), bf16),
             pltpu.VMEM((2, h, units), f32),
             pltpu.VMEM((2, heads // 2, block), f32),
-            pltpu.VMEM((2, h + 16, qkv), f32),
+            pltpu.VMEM((2, h, qkv), f32),
+            pltpu.VMEM((8, 2 * block), f32),
             pltpu.VMEM((3, 2, h, units), bf16),
             pltpu.VMEM((3, 2, h, units), bf16),
             pltpu.VMEM((2, 2, heads // 2, block), bf16),
             pltpu.VMEM((2, 2, heads // 2, block), bf16),
-            pltpu.VMEM((2, 2, h + 16, qkv), bf16),
-            pltpu.VMEM((2, 2, h + 16, qkv), bf16),
+            pltpu.VMEM((2, 2, h, qkv), bf16),
+            pltpu.VMEM((2, 2, h, qkv), bf16),
+            pltpu.VMEM((2, 2, 8, 2 * block), f32),
+            pltpu.VMEM((2, 2, 8, 2 * block), f32),
             pltpu.VMEM((8, width), f32),
-            pltpu.VMEM((2, 8, width), f32),
+            pltpu.VMEM((4, 8, 2 * block), f32),
             pltpu.VMEM((n, 16, qkv), bf16),
-            pltpu.SemaphoreType.DMA((6, 2, n - 1)),
-            pltpu.SemaphoreType.DMA((6, 2, n - 1)),
-            pltpu.SemaphoreType.DMA((3, 3, 2)),
-            pltpu.SemaphoreType.DMA((3, 3, 2)),
+            pltpu.VMEM((n, 16, 2 * block), f32),
+            pltpu.SemaphoreType.DMA((7, 2, n - 1)),
+            pltpu.SemaphoreType.DMA((7, 2, n - 1)),
+            pltpu.SemaphoreType.DMA((4, 4, 2)),
+            pltpu.SemaphoreType.DMA((4, 4, 2)),
             pltpu.SemaphoreType.DMA((80,)),
             pltpu.SemaphoreType.DMA((80,)),
             pltpu.SemaphoreType.REGULAR((2,)),
             pltpu.SemaphoreType.DMA((160,)),
         ],
         compiler_params=pltpu.CompilerParams(collective_id=2, has_side_effects=True, vmem_limit_bytes=62 * 2**20),
-    )(g, n2, n1, x, to_gate, to_up, inner, grad_down, w_qkv, w_out, w_gate, w_up, w_down, q, kv, ob, hid, lse, cs, sn, start)
+    )(g, n2, n1, x, to_gate, to_up, inner, *grads, w_qkv, w_out, w_gate, w_up, w_down, q, kv, ob, hid, lse, cs, sn, start)
 
 
 def prep_kernel(q_ref, k_ref, v_ref, d_ref, g1_ref, g2_ref, qkv_ref, dt_ref):
@@ -1096,25 +1254,25 @@
     sn = jnp.concatenate([-sine, sine, -sine, sine], axis=1)
 
     p_qkv, p_down = prep(w_query, w_key, w_value, w_down, gain_attn, gain_mlp)
-    w_qkv, w_out_all, w_g, w_u, w_d, n1, q, kv, ob, lse, hidden, n2, to_gate, to_up, inner, grad_down = forward(
+    w_qkv, w_out_all, w_g, w_u, w_d, n1, q, kv, ob, lse, hidden, n2, to_gate, to_up, inner, *grads = forward(
         n_dp, p_qkv, w_out, w_gate, w_up, p_down, tokens, cotangent, cs, sn, start[:, None]
     )
-    output, grad_tokens, s_down, s_gate, s_up, s_out, s_qkv = backward(
-        n_dp, cotangent, n2, n1, tokens, to_gate, to_up, inner, grad_down, w_qkv, w_out_all, w_g, w_u, w_d,
+    output, grad_tokens, s_down, s_gate, s_up, s_out, s_qkv, s_gain = backward(
+        n_dp, cotangent, n2, n1, tokens, to_gate, to_up, inner, grads, w_qkv, w_out_all, w_g, w_u, w_d,
         q, kv, ob, hidden, lse, cs, sn, start[None, :]
-    )[:7]
+    )[:8]
     return (
         output,
         grad_tokens.astype(f32),
-        s_qkv[:block, :cols],
-        s_qkv[:block, cols : cols + HD],
-        s_qkv[:block, cols + HD :],
+        s_qkv[:, :cols],
+        s_qkv[:, cols : cols + HD],
+        s_qkv[:, cols + HD :],
         s_out,
         s_gate,
         s_up,
         s_down.T,
-        s_qkv[block, :block],
-        s_qkv[block, block : 2 * block],
+        s_gain[0, :block],
+        s_gain[0, block:],
     )
 
 

time: 594 us -> 536 us (0.902)
  Pallas kernels: 548 us -> 489 us
    pallas_call x1, Pallas kernels: 326 us -> 255 us  [backward(): pl.pallas_call(functools.partial(backward_kernel, n), out_shape=(hbm((tok...]
    pallas_call x1, Pallas kernels: 221 us -> 234 us  [forward(): pl.pallas_call(functools.partial(forward_kernel, n), out_shape=tuple((jax...]
where the time goes in v1:
time: 536 us; the launch traced here: 525 us
  Pallas kernels  489 us (91%)
  local copies, waits for them, and re-layouts  22.2 us (4%)
  other arithmetic  13.2 us (2%)
    pallas_call x1, Pallas kernels, backward(): pl.pallas_call(functools.partial(backward_kernel, n), out_shape=(hbm((tok...  255 us
    pallas_call x1, Pallas kernels, forward(): pl.pallas_call(functools.partial(forward_kernel, n), out_shape=tuple((jax...  234 us
    unnamed x27, local copies, waits for them, and re-layouts  15 us

profile of v1, /device:TPU:0, one launch (start us, length us, event | category | flops | bytes accessed | tf_op | source)
XLA Modules:
  0.0 525.2 jit_solution(9662832230505781369)
XLA Ops:
  0.6 0.8 reduce-window.4
  1.5 0.7 fusion.2
  2.1 0.7 reshape.51.g1_ref
  2.8 0.7 reshape.52.g2_ref
  3.5 0.1 select_reduce_fusion
  3.6 0.6 broadcast_in_dim.13.start_ref
  4.2 0.9 copy.40.k_ref
  5.0 0.9 copy.41.v_ref
  5.9 1.0 reduce_sum.13.start_ref
  6.9 0.0 copy-start
  6.9 1.1 copy-done
  8.1 0.0 copy-start.3
  8.1 0.9 copy-done.3
  9.0 0.3 shard_map.203
  9.3 0.0 copy-start.1
  9.3 0.8 copy-done.1
  10.2 0.0 copy-start.2
  10.2 0.7 copy-done.2
  10.9 2.1 fusion
  13.0 2.0 pad_maximum_fusion
  15.0 233.8 %shard_map.204 = (bf16[8,272,640]{2,1,0:T(8,128)(2,1)}, bf16[8,512,256]{2,1,0:T(8,128)(2,1)}, bf16[8,256,1408]{2,1,0:T(8,128)(2,1)}, bf16[8,256,1408]{2,1,0:T(8,...) custom-call(bf16[272,640]{1,0:T(8,128)(2,1)} %copy-done.2, ...), custom_call_target="tpu_custom_call" | custom-call | tf_op jit(solution)/shard_map/pallas_call | solution.py:495
  248.8 254.8 %shard_map.205 = (bf16[1152,2048]{1,0:T(8,128)(2,1)}, bf16[1152,2048]{1,0:T(8,128)(2,1)}, f32[256,1408]{1,0:T(8,128)}, f32[256,1408]{1,0:T(8,128)}, f32[256,1408...) custom-call(bf16[1152,2048]{1,0:T(8,128)(2,1)} %g_hbm.1, ...), custom_call_target="tpu_custom_call" | custom-call | tf_op jit(solution)/shard_map/pallas_call | solution.py:1133
  503.7 1.3 fusion.4
  505.0 1.1 fusion.3
  506.1 1.9 slice.15
  507.9 0.7 copy.45
  508.6 0.7 copy.44
  509.4 0.0 slice-start
  509.4 3.0 copy.46
  512.3 0.0 slice-start.1
  512.3 7.5 %convert_element_type.11 = f32[1152,2048]{1,0:T(8,128)} convert(bf16[1152,2048]{1,0:T(8,128)(2,1)} %get-tuple-element.62) | non-fusion elementwise | flops 2359296 | bytes 14155776 | tf_op jit(solution)/shard_map/convert_element_type | solution.py:1266
  519.8 0.0 slice-done
  519.8 0.0 slice-done.1
  519.8 0.0 copy-start.6
  519.8 0.0 copy-start.5
  519.8 2.3 copy.51
  522.0 0.0 copy-done.6
  522.0 0.0 copy-start.4
  522.1 0.8 copy.52
  522.8 0.0 copy-done.5
  522.8 1.1 copy.53
  523.9 0.0 copy-done.4
  524.0 1.1 copy.54
  (3 shorter events, 0.0 us)
Async XLA Ops:
  6.9 1.1 copy-start
  8.1 0.9 copy-start.3
  9.3 0.9 copy-start.1
  10.2 0.7 copy-start.2
  509.4 10.4 %slice-start = ((s8[4718592]{0:T(1024)(128)(4,1)}), s8[524288]{0:T(1024)(128)(4,1)S(1)}, s32[]{:S(2)}) async-start(s8[4718592]{0:T(1024)(128)(4,1)} %bitcast.11), calls=%async_computation | async-start | bytes 1048576
  512.3 7.5 %slice-start.1 = ((s8[4718592]{0:T(1024)(128)(4,1)}), s8[4194304]{0:T(1024)(128)(4,1)S(1)}, s32[]{:S(2)}) async-start(s8[4718592]{0:T(1024)(128)(4,1)} %bitcast.11), calls=%async_computation.1 | async-start | bytes 8388608
  519.8 2.3 copy-start.6
  519.8 3.1 copy-start.5
  522.0 1.9 copy-start.4

commit v2 on v1

--- a/solution.py
+++ b/solution.py
@@ -429,8 +429,7 @@
             value = mm_nt(dg[...], blocks[j % 2, 0].reshape(256, early))
             sums[j % 2] = value + mm_nt(du[...], blocks[j % 2, 1].reshape(256, early))
             writes.append(copy(sums.at[j % 2], dn2_out.at[j]))
-            if j % 2 == 1:
-                ring.pass_on()
+            ring.pass_on()
         for made in writes[-2:]:
             made.wait()
         early_writes = [copy(dg, dg_out), copy(du, du_out)]

time: 536 us -> 536 us (level)
  no operation moved by 1% of the time
where the time goes in v2:
time: 536 us; the launch traced here: 526 us
  Pallas kernels  489 us (91%)
  local copies, waits for them, and re-layouts  22.2 us (4%)
  other arithmetic  13.2 us (2%)
    pallas_call x1, Pallas kernels, backward(): pl.pallas_call(functools.partial(backward_kernel, n), out_shape=(hbm((tok...  255 us
    pallas_call x1, Pallas kernels, forward(): pl.pallas_call(functools.partial(forward_kernel, n), out_shape=tuple((jax...  234 us
    unnamed x27, local copies, waits for them, and re-layouts  15 us

profile of v2, /device:TPU:0, one launch (start us, length us, event | category | flops | bytes accessed | tf_op | source)
XLA Modules:
  0.0 525.6 jit_solution(12181568215971884146)
XLA Ops:
  0.6 0.8 reduce-window.4
  1.5 0.7 fusion.2
  2.1 0.7 reshape.51.g1_ref
  2.8 0.7 reshape.52.g2_ref
  3.5 0.1 select_reduce_fusion
  3.6 0.6 broadcast_in_dim.13.start_ref
  4.2 0.9 copy.40.k_ref
  5.0 0.9 copy.41.v_ref
  5.9 1.0 reduce_sum.13.start_ref
  6.9 0.0 copy-start
  6.9 1.1 copy-done
  8.1 0.0 copy-start.3
  8.1 0.9 copy-done.3
  9.0 0.3 shard_map.203
  9.3 0.0 copy-start.1
  9.3 0.8 copy-done.1
  10.2 0.0 copy-start.2
  10.2 0.7 copy-done.2
  10.9 2.1 fusion
  13.0 2.0 pad_maximum_fusion
  15.0 234.0 %shard_map.204 = (bf16[8,272,640]{2,1,0:T(8,128)(2,1)}, bf16[8,512,256]{2,1,0:T(8,128)(2,1)}, bf16[8,256,1408]{2,1,0:T(8,128)(2,1)}, bf16[8,256,1408]{2,1,0:T(8,...) custom-call(bf16[272,640]{1,0:T(8,128)(2,1)} %copy-done.2, ...), custom_call_target="tpu_custom_call" | custom-call | tf_op jit(solution)/shard_map/pallas_call | solution.py:494
  249.0 255.1 %shard_map.205 = (bf16[1152,2048]{1,0:T(8,128)(2,1)}, bf16[1152,2048]{1,0:T(8,128)(2,1)}, f32[256,1408]{1,0:T(8,128)}, f32[256,1408]{1,0:T(8,128)}, f32[256,1408...) custom-call(bf16[1152,2048]{1,0:T(8,128)(2,1)} %g_hbm.1, ...), custom_call_target="tpu_custom_call" | custom-call | tf_op jit(solution)/shard_map/pallas_call | solution.py:1132
  504.1 1.3 fusion.4
  505.3 1.1 fusion.3
  506.4 1.9 slice.15
  508.3 0.7 copy.45
  509.0 0.7 copy.44
  509.7 0.0 slice-start
  509.7 3.0 copy.46
  512.7 0.0 slice-start.1
  512.7 7.5 %convert_element_type.11 = f32[1152,2048]{1,0:T(8,128)} convert(bf16[1152,2048]{1,0:T(8,128)(2,1)} %get-tuple-element.62) | non-fusion elementwise | flops 2359296 | bytes 14155776 | tf_op jit(solution)/shard_map/convert_element_type | solution.py:1265
  520.1 0.0 slice-done
  520.1 0.0 slice-done.1
  520.1 0.0 copy-start.6
  520.1 0.0 copy-start.5
  520.2 2.3 copy.51
  522.4 0.0 copy-done.6
  522.4 0.0 copy-start.4
  522.4 0.8 copy.52
  523.2 0.0 copy-done.5
  523.2 1.1 copy.53
  524.3 0.0 copy-done.4
  524.3 1.1 copy.54
  (3 shorter events, 0.0 us)
Async XLA Ops:
  6.9 1.1 copy-start
  8.1 0.9 copy-start.3
  9.3 0.9 copy-start.1
  10.2 0.7 copy-start.2
  509.7 10.4 %slice-start = ((s8[4718592]{0:T(1024)(128)(4,1)}), s8[524288]{0:T(1024)(128)(4,1)S(1)}, s32[]{:S(2)}) async-start(s8[4718592]{0:T(1024)(128)(4,1)} %bitcast.11), calls=%async_computation | async-start | bytes 1048576
  512.7 7.5 %slice-start.1 = ((s8[4718592]{0:T(1024)(128)(4,1)}), s8[4194304]{0:T(1024)(128)(4,1)S(1)}, s32[]{:S(2)}) async-start(s8[4718592]{0:T(1024)(128)(4,1)} %bitcast.11), calls=%async_computation.1 | async-start | bytes 8388608
  520.1 2.3 copy-start.6
  520.1 3.1 copy-start.5
  522.4 1.9 copy-start.4
